TPU v7x, 32 devices: a whole 2x2x4 slice. The times are simulated.
32 devices in a mesh: ctx: 8 (over z, x), wa: 4 (over y, core).
Axes of the slice: x: 2, y: 2, z: 4, core: 2. Of those that a mesh axis runs over, the one named last changes fastest.
Arguments:
- tokens: bfloat16 [4, 1024, 1536], P('wa', 'ctx'), may hold values from -6 to 6
- teacher: float32 [4, 1024, 1536], P('wa', 'ctx'), may hold values from -6 to 6
- lengths: int32 [4], replicated, may hold values from 897 to 1024, as said below
- routes: int32 [4, 1024, 6], P('wa', 'ctx'), may hold values from 0 to 15, all different within a row; in each aligned block of 128 rows (0 to 127, 128 to 255, ..., all dimensions but the last counted through in order) at most 96 rows name the same one
- query_weight: bfloat16 [1536, 1536], P('wa'), may hold values from -0.15625 to 0.15625
- key_projection_matrix: bfloat16 [1536, 512], P('wa'), may hold values from -0.15625 to 0.15625
- value_projection_matrix: bfloat16 [1536, 512], P('wa'), may hold values from -0.15625 to 0.15625
- output_weight: bfloat16 [1536, 1536], P('wa'), may hold values from -0.4375 to 0.4375
- attn_gain: bfloat16 [1536], P('wa'), may hold values from 0.5 to 1.5
- moe_gain: bfloat16 [1536], P('wa'), may hold values from 0.5 to 1.5
- router_weight: bfloat16 [1536, 16], P('wa'), may hold values from -0.078125 to 0.078125
- shared_gate: bfloat16 [1536, 1024], P('wa'), may hold values from -0.15625 to 0.15625
- shared_up: bfloat16 [1536, 1024], P('wa'), may hold values from -0.15625 to 0.15625
- shared_down: bfloat16 [1536, 1024], P('wa'), may hold values from -0.1875 to 0.1875
- expert_gate: bfloat16 [16, 1536, 512], P('wa'), may hold values from -0.15625 to 0.15625
- expert_up: bfloat16 [16, 1536, 512], P('wa'), may hold values from -0.15625 to 0.15625
- expert_down: bfloat16 [16, 1536, 512], P('wa'), may hold values from -0.25 to 0.25
Outputs:
- block_out: bfloat16 [4, 1024, 1536], P('wa', 'ctx')
- grad_tokens: float32 [4, 1024, 1536], P('wa', 'ctx')
- grad_query: float32 [1536, 1536], P(('ctx', 'wa'))
- grad_key: float32 [1536, 512], P(('ctx', 'wa'))
- grad_value: float32 [1536, 512], P(('ctx', 'wa'))
- grad_output: float32 [1536, 1536], P(('ctx', 'wa'))
- grad_attn_gain: float32 [1536], P(('ctx', 'wa'))
- grad_moe_gain: float32 [1536], P(('ctx', 'wa'))
- grad_router: float32 [1536, 16], P(('ctx', 'wa'))
- grad_shared_gate: float32 [1536, 1024], P(('ctx', 'wa'))
- grad_shared_up: float32 [1536, 1024], P(('ctx', 'wa'))
- grad_shared_down: float32 [1536, 1024], P(('ctx', 'wa'))
- grad_expert_gate: float32 [16, 1536, 512], P('wa', 'ctx')
- grad_expert_up: float32 [16, 1536, 512], P('wa', 'ctx')
- grad_expert_down: float32 [16, 1536, 512], P('wa', 'ctx')
- loss: float32 [], replicated
Inputs may be any that keep to these rules, and one draw needn't show every extreme that they name: `lengths`: every sequence reaches into the last block of 128 positions; one is exactly 1024 long. `routes`: a position names 6 different experts; within the 128 positions of one device no expert is named more than 96 times, a bound that some block reaches.
All inputs are finite; a program needn't handle non-finite values.
Results may differ from a plain program's by a relative error of at most 0.029.
Values may be sent and summed in bfloat16 or wider, within the bound.
No kernel may reach another device: no remote copies, remote signals or barrier semaphores. Data moves between devices by JAX's collectives and lax.ppermute only.
A program may use at most 320 MiB of HBM per device.

v0:
```python
import jax
import jax.numpy as jnp
from jax import lax
from jax.experimental import pallas as pl
from jax.experimental.pallas import tpu as pltpu
from jax.sharding import PartitionSpec as P

QUERY_HEADS = 12
KEY_VALUE_HEADS = 4
HEAD_SIZE = 128
TOP = 6
GROUP = QUERY_HEADS // KEY_VALUE_HEADS

epsilon = 1e-06
masked = -1e30
bf16 = jnp.bfloat16
f32 = jnp.float32


def dot(a, b, dims):
    return lax.dot_general(a, b, ((dims[0], dims[1]), ((), ())), preferred_element_type=f32)


def mm(a, b):
    return dot(a, b, ((1,), (0,)))


def mm_nt(a, b):
    return dot(a, b, ((1,), (1,)))


def mm_tn(a, b):
    return dot(a, b, ((0,), (0,)))


def swap(value, axis, bit):
    size = lax.axis_size(axis)
    return lax.ppermute(value, axis, [(i, i ^ bit) for i in range(size)])


def perm4(parts, w):
    core, upper = w % 2 == 1, w // 2 == 1
    a, b, c, d = parts
    a, b, c, d = (
        jnp.where(core, b, a),
        jnp.where(core, a, b),
        jnp.where(core, d, c),
        jnp.where(core, c, d),
    )
    return [
        jnp.where(upper, c, a),
        jnp.where(upper, d, b),
        jnp.where(upper, a, c),
        jnp.where(upper, b, d),
    ]


def gather_wa(value):
    near = swap(value, "wa", 1)
    far = swap(value, "wa", 2)
    return [value, near, far, swap(far, "wa", 1)]


def silu_parts(rows):
    sigma = jax.nn.sigmoid(rows)
    return rows * sigma, sigma * (1.0 + rows * (1.0 - sigma))


def rms_factor(rows):
    return lax.rsqrt(jnp.mean(rows * rows, axis=-1, keepdims=True) + epsilon)


def norm_backward(rows, factor, gain, upstream):
    weighted = upstream * gain
    inner = jnp.mean(weighted * rows, axis=-1, keepdims=True)
    grad = factor * weighted - rows * (factor * factor * factor * inner)
    return grad, jnp.sum(upstream * rows * factor, axis=0)


def gather_keys(kv, c, n):
    rows = kv.shape[0]
    if n > 8:
        return lax.all_gather(kv, "ctx", axis=0, tiled=True), jnp.arange(n * rows)
    levels = [kv]
    for s in range(1, n // 2):
        levels.append(lax.ppermute(kv, "ctx", [(i, i + 2 * s) for i in range(n - 2 * s)]))
    blocks, pos = [], []
    for s, level in enumerate(levels):
        blocks += [level, swap(level, "ctx", 1)]
        start = (c - 2 * s) * rows
        pos += [start + jnp.arange(rows), (c - 2 * s + 1 - 2 * (c % 2)) * rows + jnp.arange(rows)]
    return jnp.concatenate(blocks), jnp.concatenate(pos)


def scatter_keys(grads, n):
    rows = grads.shape[0] // n
    if n > 8:
        return lax.psum_scatter(grads, "ctx", scatter_dimension=0, tiled=True).astype(f32)
    blocks = grads.reshape(n, rows, -1)
    total = None
    for s in reversed(range(n // 2)):
        level = blocks[2 * s].astype(f32) + swap(blocks[2 * s + 1], "ctx", 1).astype(f32)
        if s:
            level = lax.ppermute(
                level.astype(bf16), "ctx", [(i + 2 * s, i) for i in range(n - 2 * s)]
            ).astype(f32)
        total = level if total is None else total + level
    return total


def heads(rows, groups):
    return rows.reshape(rows.shape[0], KEY_VALUE_HEADS, groups, HEAD_SIZE)


def attention_scores(q, k, pos, qpos, length):
    scale = HEAD_SIZE**-0.5
    scores = jnp.einsum("tkgd,nkd->kgtn", q, k, preferred_element_type=f32) * scale
    allowed = (pos[None, :] >= 0) & (pos[None, :] <= qpos[:, None]) & (pos[None, :] < length)
    return scores, allowed


def chunked(kv, pos):
    size = 1024
    if kv.shape[0] <= size:
        return None
    return kv.reshape(-1, size, kv.shape[1]), pos.reshape(-1, size)


def attention_forward(q, kv, pos, qpos, length):
    rows = q.shape[0]
    pieces = chunked(kv, pos)
    width = KEY_VALUE_HEADS * HEAD_SIZE
    if pieces is None:
        k, v = heads(kv[:, :width], 1)[:, :, 0], heads(kv[:, width:], 1)[:, :, 0]
        scores, allowed = attention_scores(q, k, pos, qpos, length)
        scores = jnp.where(allowed, scores, masked)
        top = jnp.max(scores, axis=-1, keepdims=True)
        weights = jnp.exp(scores - top)
        probs = (weights / jnp.sum(weights, axis=-1, keepdims=True)).astype(bf16)
        attn = jnp.einsum("kgtn,nkd->tkgd", probs, v, preferred_element_type=f32)
        return attn, probs

    def step(carry, piece):
        top, total, accum = carry
        kv_now, pos_now = piece
        k, v = heads(kv_now[:, :width], 1)[:, :, 0], heads(kv_now[:, width:], 1)[:, :, 0]
        scores, allowed = attention_scores(q, k, pos_now, qpos, length)
        scores = jnp.where(allowed, scores, masked)
        new_top = jnp.maximum(top, jnp.max(scores, axis=-1, keepdims=True))
        weights = jnp.where(allowed, jnp.exp(scores - new_top), 0.0)
        shrink = jnp.exp(top - new_top)
        total = total * shrink + jnp.sum(weights, axis=-1, keepdims=True)
        update = jnp.einsum("kgtn,nkd->kgtd", weights.astype(bf16), v, preferred_element_type=f32)
        return (new_top, total, accum * shrink + update), None

    shape = (KEY_VALUE_HEADS, GROUP, rows)
    start = (
        jnp.full(shape + (1,), masked, f32),
        jnp.zeros(shape + (1,), f32),
        jnp.zeros(shape + (HEAD_SIZE,), f32),
    )
    (top, total, accum), _ = lax.scan(step, start, pieces)
    return jnp.transpose(accum / total, (2, 0, 1, 3)), top + jnp.log(total)


def attention_backward(q, kv, pos, qpos, length, kept, d_attn, delta):
    scale = HEAD_SIZE**-0.5
    width = KEY_VALUE_HEADS * HEAD_SIZE

    def terms(probs, k, v):
        d_probs = jnp.einsum("tkgd,nkd->kgtn", d_attn, v, preferred_element_type=f32)
        d_scores = (probs.astype(f32) * (d_probs - delta)).astype(bf16)
        d_q = jnp.einsum("kgtn,nkd->tkgd", d_scores, k, preferred_element_type=f32) * scale
        d_k = jnp.einsum("kgtn,tkgd->nkd", d_scores, q, preferred_element_type=f32) * scale
        d_v = jnp.einsum(
            "kgtn,tkgd->nkd", probs.astype(bf16), d_attn, preferred_element_type=f32
        )
        keys = k.shape[0]
        return d_q, jnp.concatenate(
            [d_k.reshape(keys, width), d_v.reshape(keys, width)], axis=1
        ).astype(bf16)

    pieces = chunked(kv, pos)
    if pieces is None:
        k, v = heads(kv[:, :width], 1)[:, :, 0], heads(kv[:, width:], 1)[:, :, 0]
        return terms(kept, k, v)

    def step(d_q, piece):
        kv_now, pos_now = piece
        k, v = heads(kv_now[:, :width], 1)[:, :, 0], heads(kv_now[:, width:], 1)[:, :, 0]
        scores, allowed = attention_scores(q, k, pos_now, qpos, length)
        probs = jnp.where(allowed, jnp.exp(scores - kept), 0.0)
        more, d_kv = terms(probs, k, v)
        return d_q + more, d_kv

    d_q, d_kv = lax.scan(step, jnp.zeros(q.shape, f32), pieces)
    return d_q, d_kv.reshape(kv.shape)


EXTRA = 128
in_vmem = pl.BlockSpec(memory_space=pltpu.VMEM)
in_smem = pl.BlockSpec(memory_space=pltpu.SMEM)
anywhere = pl.BlockSpec(memory_space=pltpu.MemorySpace.HBM)


def hbm(shape, dtype):
    return pltpu.HBM(shape, dtype)


def in_hbm(value):
    return pltpu.with_memory_space_constraint(value, pltpu.HBM)


def start_copy(source, target, sems, index):
    copy = pltpu.make_async_copy(source, target, sems.at[index])
    copy.start()
    return copy


def cost(microseconds):
    return pl.CostEstimate(flops=int(microseconds * 1.15e+09), bytes_accessed=0, transcendentals=0)


def limits(mib):
    return pltpu.CompilerParams(vmem_limit_bytes=mib << 20)


def split_low(value, lane, shift):
    high = value.astype(bf16).astype(f32)
    rest = pltpu.roll(value - high, shift, 1)
    return jnp.where(lane < shift, high, jnp.where(lane < 2 * shift, rest, 0.0))


def join_low(value, lane, shift):
    total = value + pltpu.roll(value, value.shape[1] - shift, 1)
    return jnp.where(lane < shift, total, 0.0)


def lanes_of(rows):
    return lax.broadcasted_iota(jnp.int32, (rows, EXTRA), 1)


def load_rows(sources, rows_ref, extra_ref, sems, first):
    features, copies = rows_ref.shape[1], []
    for i, source in enumerate(sources):
        at = pl.ds(i * source.shape[0], source.shape[0])
        copies.append(
            start_copy(source.at[:, pl.ds(0, features)], rows_ref.at[at], sems, first + 2 * i)
        )
        if extra_ref is not None:
            lanes = pl.ds(features, EXTRA)
            copies.append(
                start_copy(source.at[:, lanes], extra_ref.at[at], sems, first + 2 * i + 1)
            )
    return copies


def wait_all(copies):
    for copy in copies:
        copy.wait()


def attention_kernel(info_ref, q_ref, *refs):
    blocks = len(refs) - 6
    kv_refs, (out_ref, attn_out, probs_out, attn_ref, probs_ref, sems) = refs[:blocks], refs[blocks:]
    sent = []
    rows = q_ref.shape[0]
    width = KEY_VALUE_HEADS * HEAD_SIZE
    qpos = info_ref[0] * rows + lax.broadcasted_iota(jnp.int32, (rows, rows), 0)
    biases = []
    for b in range(blocks):
        kpos = info_ref[2 + b] + lax.broadcasted_iota(jnp.int32, (rows, rows), 1)
        allowed = (kpos >= 0) & (kpos <= qpos) & (kpos < info_ref[1])
        bias = jnp.where(allowed, 0.0, masked)
        biases.append(jnp.concatenate([bias] * GROUP, axis=0))
    for k in range(KEY_VALUE_HEADS):
        first = k * GROUP * HEAD_SIZE
        q = jnp.concatenate(
            [q_ref[:, first + g * HEAD_SIZE : first + (g + 1) * HEAD_SIZE] for g in range(GROUP)],
            axis=0,
        )
        cols = slice(k * HEAD_SIZE, (k + 1) * HEAD_SIZE)
        scores = [
            mm_nt(q, kv_refs[b][:, cols]) * HEAD_SIZE**-0.5 + biases[b] for b in range(blocks)
        ]
        top = scores[0]
        for score in scores[1:]:
            top = jnp.maximum(top, score)
        top = jnp.max(top, axis=1, keepdims=True)
        weights = [jnp.exp(score - top) for score in scores]
        total = weights[0]
        for weight in weights[1:]:
            total = total + weight
        scale = 1.0 / jnp.sum(total, axis=1, keepdims=True)
        attn = None
        for b in range(blocks):
            probs = (weights[b] * scale).astype(bf16)
            probs_ref[k, b] = probs
            term = mm(probs, kv_refs[b][:, width + k * HEAD_SIZE : width + (k + 1) * HEAD_SIZE])
            attn = term if attn is None else attn + term
        sent.append(start_copy(probs_ref.at[k], probs_out.at[k], sems, k))
        for g in range(GROUP):
            at = slice(first + g * HEAD_SIZE, first + (g + 1) * HEAD_SIZE)
            attn_ref[:, at] = attn[g * rows : (g + 1) * rows]
            out_ref[:, at] = attn[g * rows : (g + 1) * rows].astype(bf16)
    sent.append(start_copy(attn_ref, attn_out, sems, KEY_VALUE_HEADS))
    wait_all(sent)


def attention_call(info, q, kv_blocks):
    rows, blocks = q.shape[0], len(kv_blocks)
    probs = (KEY_VALUE_HEADS, blocks, GROUP * rows, rows)
    return pl.pallas_call(
        attention_kernel,
        out_shape=(jax.ShapeDtypeStruct(q.shape, bf16), hbm(q.shape, f32), hbm(probs, bf16)),
        in_specs=[in_smem] + [in_vmem] * (1 + blocks),
        out_specs=(in_vmem, anywhere, anywhere),
        scratch_shapes=[
            pltpu.VMEM(q.shape, f32),
            pltpu.VMEM(probs, bf16),
            pltpu.SemaphoreType.DMA((KEY_VALUE_HEADS + 1,)),
        ],
        compiler_params=limits(12),
        cost_estimate=cost(5),
        name="attention_forward",
    )(info, q, *kv_blocks)


def attention_back_kernel(d_ref, q_in, attn_in, probs_in, *refs):
    blocks = (len(refs) - 6) // 2
    kv_in, refs = refs[:blocks], refs[blocks:]
    dq_ref, refs = refs[0], refs[1:]
    own_refs, pair_refs, refs = refs[: blocks // 2], refs[blocks // 2 : blocks], refs[blocks:]
    q_ref, attn_ref, probs_ref, kv_ref, sems = refs
    rows = q_ref.shape[0]
    width = KEY_VALUE_HEADS * HEAD_SIZE
    scale = HEAD_SIZE**-0.5
    loads = [start_copy(q_in, q_ref, sems, 0), start_copy(attn_in, attn_ref, sems, 1)]
    loads += [start_copy(kv_in[b], kv_ref.at[b], sems, 2 + b) for b in range(blocks)]
    probs_loads = [
        start_copy(probs_in.at[k], probs_ref.at[k], sems, 2 + blocks + k)
        for k in range(KEY_VALUE_HEADS)
    ]
    wait_all(loads)

    def stacked(ref, first):
        return jnp.concatenate(
            [ref[:, first + g * HEAD_SIZE : first + (g + 1) * HEAD_SIZE] for g in range(GROUP)],
            axis=0,
        )

    for k in range(KEY_VALUE_HEADS):
        first = k * GROUP * HEAD_SIZE
        q, d_attn = stacked(q_ref, first), stacked(d_ref, first)
        delta = jnp.sum(d_attn.astype(f32) * stacked(attn_ref, first), axis=1, keepdims=True)
        kcols = slice(k * HEAD_SIZE, (k + 1) * HEAD_SIZE)
        vcols = slice(width + k * HEAD_SIZE, width + (k + 1) * HEAD_SIZE)
        probs_loads[k].wait()
        d_q = None
        for b in range(blocks):
            key, value = kv_ref[b, :, kcols], kv_ref[b, :, vcols]
            probs = probs_ref[k, b]
            d_probs = mm_nt(d_attn, value)
            d_scores = (probs.astype(f32) * (d_probs - delta)).astype(bf16)
            term = mm(d_scores, key)
            d_q = term if d_q is None else d_q + term
            level = b // 2
            target = own_refs[level] if b % 2 == 0 else pair_refs[level]
            target[:, kcols] = (mm_tn(d_scores, q) * scale).astype(bf16)
            target[:, vcols] = mm_tn(probs, d_attn).astype(bf16)
        d_q = (d_q * scale).astype(bf16)
        for g in range(GROUP):
            dq_ref[:, first + g * HEAD_SIZE : first + (g + 1) * HEAD_SIZE] = d_q[
                g * rows : (g + 1) * rows
            ]


def attention_back_call(d_attn, q, attn, probs, kv_blocks):
    blocks = len(kv_blocks)
    kv_shape = kv_blocks[0].shape
    done = pl.pallas_call(
        attention_back_kernel,
        out_shape=(jax.ShapeDtypeStruct(q.shape, bf16),)
        + (jax.ShapeDtypeStruct(kv_shape, bf16),) * blocks,
        in_specs=[in_vmem] + [anywhere] * (3 + blocks),
        out_specs=(in_vmem,) * (1 + blocks),
        scratch_shapes=[
            pltpu.VMEM(q.shape, bf16),
            pltpu.VMEM(q.shape, f32),
            pltpu.VMEM(probs.shape, bf16),
            pltpu.VMEM((blocks,) + kv_shape, bf16),
            pltpu.SemaphoreType.DMA((2 + blocks + KEY_VALUE_HEADS,)),
        ],
        compiler_params=limits(16),
        cost_estimate=cost(10),
        name="attention_backward",
    )(d_attn, in_hbm(q), in_hbm(attn), in_hbm(probs), *[in_hbm(value) for value in kv_blocks])
    return done[0], list(done[1 : 1 + blocks // 2]), list(done[1 + blocks // 2 :])


def out_halves(info_ref, size):
    half = info_ref[2]
    return (
        pl.ds(pl.multiple_of(half * size, 128), size),
        pl.ds(pl.multiple_of((1 - half) * size, 128), size),
    )


def branch_kernel(
    info_ref, attn_ref, o0, o1, o2, o3, tok_ref, gain_ref, router_ref, routes_ref,
    resid_out, ext_ref, gates_ref, resid_ref, sems,
):
    rows, features = tok_ref.shape
    slab = o0.shape[0]
    here, other = out_halves(info_ref, o2.shape[1])
    attn = attn_ref[...]
    for i in range(4):
        if i < 2:
            term = mm_nt(attn, (o0, o1)[i][...])
        else:
            part = (o2, o3)[i - 2]
            term = mm_nt(attn_ref[:, here], part[:slab]) + mm_nt(attn_ref[:, other], part[slab:])
        at = pl.ds(pl.multiple_of((info_ref[0] ^ i) * slab, 128), slab)
        resid_ref[:, at] = tok_ref[:, at].astype(f32) + term
    sent = start_copy(resid_ref, resid_out, sems, 0)
    resid = resid_ref[...]
    moe_in = (resid * rms_factor(resid) * gain_ref[...]).astype(bf16)
    logits = mm_nt(moe_in, router_ref[...])
    lane = lanes_of(rows)
    chosen = lane == routes_ref[:, 0:1]
    for t in range(1, routes_ref.shape[1]):
        chosen = chosen | (lane == routes_ref[:, t : t + 1])
    logits = jnp.where(chosen, logits, masked)
    raised = jnp.where(chosen, jnp.exp(logits - jnp.max(logits, axis=1, keepdims=True)), 0.0)
    gates = raised / jnp.sum(raised, axis=1, keepdims=True)
    gates_ref[...] = gates
    ext_ref[:, :features] = moe_in
    ext_ref[:, features:] = split_low(gates, lane, 16).astype(bf16)
    sent.wait()


def branch_call(info, attn, output_parts, own_tokens, gain, router, routes):
    rows, features = own_tokens.shape
    return pl.pallas_call(
        branch_kernel,
        out_shape=(
            hbm((rows, features), f32),
            jax.ShapeDtypeStruct((rows, features + EXTRA), bf16),
            jax.ShapeDtypeStruct((rows, EXTRA), f32),
        ),
        in_specs=[in_smem] + [in_vmem] * 9,
        out_specs=(anywhere, in_vmem, in_vmem),
        scratch_shapes=[pltpu.VMEM((rows, features), f32), pltpu.SemaphoreType.DMA((1,))],
        compiler_params=limits(12),
        cost_estimate=cost(4.5),
        name="branch_and_router",
    )(info, attn, *output_parts, own_tokens, gain, router, routes)


def result_kernel(info_ref, scale_ref, resid_in, own_in, teacher_in, near_ref, far_ref,
                  out_hbm, grad_hbm, ext_ref,
                  resid_ref, own_ref, teacher_ref, out_ref, grad_ref, sems):
    loads = [
        start_copy(source, target, sems, i)
        for i, (source, target) in enumerate(
            [(resid_in, resid_ref), (own_in, own_ref), (teacher_in, teacher_ref)]
        )
    ]
    rows, features = resid_ref.shape
    wait_all(loads)
    result = (
        resid_ref[...]
        + own_ref[...]
        + near_ref[...].astype(f32)
        + far_ref[...].astype(f32)
    )
    out_ref[...] = result.astype(bf16)
    sent = [start_copy(out_ref, out_hbm, sems, 3)]
    qpos = info_ref[0] * rows + lax.broadcasted_iota(jnp.int32, (rows, 1), 0)
    error = jnp.where(qpos < info_ref[1], result - teacher_ref[...], 0.0)
    grad = error * scale_ref[0]
    grad_ref[...] = grad
    sent.append(start_copy(grad_ref, grad_hbm, sems, 4))
    ext_ref[:, :features] = grad.astype(bf16)
    lane = lanes_of(rows)
    row_loss = jnp.where(lane == 0, jnp.sum(error * error, axis=1, keepdims=True), 0.0)
    ext_ref[:, features:] = split_low(row_loss, lane, 16).astype(bf16)
    wait_all(sent)


def result_call(info, scale, resid, own, near, far, teacher):
    rows, features = resid.shape
    flat = (rows, features)
    return pl.pallas_call(
        result_kernel,
        out_shape=(
            hbm(flat, bf16),
            hbm(flat, f32),
            jax.ShapeDtypeStruct((rows, features + EXTRA), bf16),
        ),
        in_specs=[in_smem] * 2 + [anywhere] * 3 + [in_vmem] * 2,
        out_specs=(anywhere, anywhere, in_vmem),
        scratch_shapes=[pltpu.VMEM(flat, f32)] * 3
        + [pltpu.VMEM(flat, bf16), pltpu.VMEM(flat, f32), pltpu.SemaphoreType.DMA((5,))],
        compiler_params=limits(12),
        cost_estimate=cost(3.5),
        name="result_and_error",
    )(info, scale, in_hbm(resid), in_hbm(own), in_hbm(teacher), near, far)


def resid_back_kernel(info_ref, far_ref, gain_ref, *refs):
    sources, refs = refs[:11], refs[11:]
    (out_hbm, gz_ref, d_attn_ref, small_ref), refs = refs[:4], refs[4:]
    held, (out_ref, sum_ref, sems) = refs[:11], refs[11:]
    loads = [
        start_copy(source, target, sems, i)
        for i, (source, target) in enumerate(zip(sources, held, strict=True))
    ]
    own_ref, near_ref, grad_ref, resid_ref, ext_ref, gates_ref, router_ref, o0, o1, o2, o3 = held
    rows, features = resid_ref.shape
    slab = o0.shape[0]
    lane = lanes_of(rows)
    tail = slice(features, features + EXTRA)
    wait_all(loads[:7])
    d_gate = join_low(
        own_ref[:, tail] + near_ref[:, tail].astype(f32) + far_ref[:, tail].astype(f32), lane, 16
    )
    gates = gates_ref[...]
    d_logits = gates * (d_gate - jnp.sum(gates * d_gate, axis=1, keepdims=True))
    d_logits = d_logits.astype(bf16)
    body = slice(0, features)
    upstream = (
        own_ref[:, body]
        + near_ref[:, body].astype(f32)
        + far_ref[:, body].astype(f32)
        + mm(d_logits, router_ref[...])
    )
    resid = resid_ref[...]
    grad_norm, grad_gain = norm_backward(resid, rms_factor(resid), gain_ref[...], upstream)
    experts = small_ref.shape[0] - 8
    small_ref[:experts, :] = mm_tn(d_logits, ext_ref[:, body])[:experts]
    small_ref[experts:, :] = jnp.broadcast_to(grad_gain[None], (8, features))
    grad_resid = grad_ref[...] + grad_norm
    out_ref[...] = grad_resid
    sent = start_copy(out_ref, out_hbm, sems, len(sources))
    gz_ref[...] = grad_resid.astype(bf16)
    gz = [
        gz_ref[:, pl.ds(pl.multiple_of((info_ref[0] ^ i) * slab, 128), slab)] for i in range(4)
    ]
    wait_all(loads[7:])
    sum_ref[...] = mm(gz[0], o0[...]) + mm(gz[1], o1[...])
    here, other = out_halves(info_ref, o2.shape[1])
    sum_ref[:, here] += mm(gz[2], o2[:slab]) + mm(gz[3], o3[:slab])
    sum_ref[:, other] += mm(gz[2], o2[slab:]) + mm(gz[3], o3[slab:])
    d_attn_ref[...] = sum_ref[...].astype(bf16)
    sent.wait()


def resid_back_call(info, own, near, far, grad, resid, ext, gates, gain, router, output_parts, experts):
    rows, features = resid.shape
    sources = [own, near, grad, resid, ext, gates, router, *output_parts]
    heads_wide = output_parts[0].shape[1]
    return pl.pallas_call(
        resid_back_kernel,
        out_shape=(
            hbm((rows, features), f32),
            jax.ShapeDtypeStruct((rows, features), bf16),
            jax.ShapeDtypeStruct((rows, heads_wide), bf16),
            jax.ShapeDtypeStruct((experts + 8, features), f32),
        ),
        in_specs=[in_smem] + [in_vmem] * 2 + [anywhere] * len(sources),
        out_specs=(anywhere,) + (in_vmem,) * 3,
        scratch_shapes=[pltpu.VMEM(value.shape, value.dtype) for value in sources]
        + [
            pltpu.VMEM((rows, features), f32),
            pltpu.VMEM((rows, heads_wide), f32),
            pltpu.SemaphoreType.DMA((len(sources) + 1,)),
        ],
        compiler_params=limits(20),
        cost_estimate=cost(5),
        name="residual_backward",
    )(info, far, gain, *[in_hbm(value) for value in sources])


def gate_column(extra, lane, expert):
    here = (lane == expert) | (lane == expert + 16)
    return jnp.sum(jnp.where(here, extra, 0.0), axis=1, keepdims=True)


def shared_parts_of(shared_ref):
    width = shared_ref.shape[1] // 3
    return [shared_ref[:, i * width : (i + 1) * width] for i in range(3)]


def experts_kernel(info_ref, xa_ref, xb_ref, gate_ref, up_ref, down_ref, shared_ref,
                   outa_hbm, outb_ref, gp_out, upre_out, hid_out,
                   gp_ref, upre_ref, hid_ref, x_ref, acc_ref, sems):
    rows, features = outb_ref.shape
    here, _, width = gate_ref.shape
    x_ref[:rows] = xa_ref[:, :features]
    x_ref[rows:] = xb_ref[:, :features]
    extra = jnp.concatenate([xa_ref[:, features:], xb_ref[:, features:]], axis=0).astype(f32)
    lane = lanes_of(2 * rows)

    def unit(gate_w, up_w):
        gate_pre, up_pre = mm(x_ref[...], gate_w), mm(x_ref[...], up_w)
        return gate_pre, up_pre, gate_pre * jax.nn.sigmoid(gate_pre) * up_pre

    s_gate, s_up, s_down = shared_parts_of(shared_ref)
    gate_pre, up_pre, hidden = unit(s_gate, s_up)
    hidden = hidden.astype(bf16)
    acc_ref[...] = mm_nt(hidden, s_down)
    part = hidden.shape[1] // 2
    for half in range(2):
        cols, mine = slice(2 * width, 2 * width + part), slice(half * part, (half + 1) * part)
        gp_ref[half, :, cols] = gate_pre[:, mine].astype(bf16)
        upre_ref[half, :, cols] = up_pre[:, mine].astype(bf16)
        hid_ref[info_ref[1] ^ half, :, cols] = hidden[:, mine]
    sent = []
    for e in range(here):
        gate = gate_column(extra, lane, info_ref[0] * here + e)
        gate_pre, up_pre, hidden = unit(gate_ref[e], up_ref[e])
        hidden = (hidden * gate).astype(bf16)
        half, at = e // 2, (e % 2) * width
        cols = slice(at, at + width)
        gp_ref[half, :, cols] = gate_pre.astype(bf16)
        upre_ref[half, :, cols] = up_pre.astype(bf16)
        hid_ref[info_ref[1] ^ half, :, cols] = hidden
        if e % 2:
            sent.append(start_copy(gp_ref.at[half], gp_out.at[half], sems, 2 * half))
            sent.append(start_copy(upre_ref.at[half], upre_out.at[half], sems, 2 * half + 1))
        if e + 1 == here:
            sent.append(start_copy(hid_ref.at[0], hid_out, sems, 4))
        acc_ref[...] += mm_nt(hidden, down_ref[e])
    outb_ref[...] = acc_ref[rows:].astype(bf16)
    sent.append(start_copy(acc_ref.at[pl.ds(0, rows)], outa_hbm, sems, 5))
    wait_all(sent)


def experts_call(info, xa, xb, weights):
    rows, features = xa.shape[0], xa.shape[1] - EXTRA
    wide = 2 * weights[0].shape[2] + weights[3].shape[1] // 6
    both, half = hbm((2, 2 * rows, wide), bf16), hbm((2 * rows, wide), bf16)
    return pl.pallas_call(
        experts_kernel,
        out_shape=(
            hbm((rows, features), f32),
            jax.ShapeDtypeStruct((rows, features), bf16),
            both,
            both,
            half,
        ),
        in_specs=[in_smem] + [in_vmem] * 6,
        out_specs=(anywhere, in_vmem) + (anywhere,) * 3,
        scratch_shapes=[pltpu.VMEM(both.shape, bf16)] * 3
        + [
            pltpu.VMEM((2 * rows, features), bf16),
            pltpu.VMEM((2 * rows, features), f32),
            pltpu.SemaphoreType.DMA((6,)),
        ],
        compiler_params=limits(16),
        cost_estimate=cost(8),
        name="experts_forward",
    )(info, xa, xb, *weights)


def hidden_back(d_hidden, gate_pre, up_pre, gate):
    gate_pre, up_pre = gate_pre.astype(f32), up_pre.astype(f32)
    act, slope = silu_parts(gate_pre)
    d_gate = None
    if gate is not None:
        d_gate = jnp.sum(d_hidden * act * up_pre, axis=1, keepdims=True)
        d_hidden = d_hidden * gate
    return d_gate, (d_hidden * up_pre * slope).astype(bf16), (d_hidden * act).astype(bf16)


def experts_back_kernel(info_ref, *refs):
    (gate_ref, up_ref, down_ref, shared_ref), refs = refs[:4], refs[4:]
    g_in, e_in, (gpa_in, gpb_in, upa_in, upb_in), refs = refs[:4], refs[4:8], refs[8:12], refs[12:]
    (dxa_hbm, dxb_ref, dxc_ref, dxd_ref, dg_out, du_out), refs = refs[:6], refs[6:]
    gp_ref, upre_ref, dg_ref, du_ref, g_ref, extra_ref, dxa_ref, acc_ref, sems = refs
    rows = g_in[0].shape[0]
    features = g_ref.shape[1]
    here, _, width = gate_ref.shape
    x = info_ref[1]
    first, last = pl.ds(0, 2 * rows), pl.ds(2 * rows, 2 * rows)
    loads = load_rows(g_in, g_ref, None, sems, 0)
    late = [
        start_copy(source, target, sems, 8 + i)
        for i, (source, target) in enumerate(
            [
                (gpa_in, gp_ref.at[:, first]),
                (gpb_in, gp_ref.at[:, last]),
                (upa_in, upre_ref.at[:, first]),
                (upb_in, upre_ref.at[:, last]),
            ]
        )
    ]
    for i in range(4):
        at = pl.ds(i * rows, rows)
        source = e_in[i].at[:, pl.ds(features, EXTRA)]
        late.append(start_copy(source, extra_ref.at[at], sems, 12 + i))
    wait_all(loads)
    s_gate, s_up, s_down = shared_parts_of(shared_ref)
    spans = [slice(i * 2 * rows, (i + 1) * 2 * rows) for i in range(2)]
    d_hiddens = [mm(g_ref[span], s_down) for span in spans]
    wait_all(late)
    lane = lanes_of(2 * rows)
    extras = [extra_ref[span].astype(f32) for span in spans]
    d_gates = [jnp.zeros((2 * rows, EXTRA), f32)] * 2
    part = d_hiddens[0].shape[1] // 2
    cols = slice(2 * width, 2 * width + part)
    for i, span in enumerate(spans):
        total = None
        for half in range(2):
            at = slice(half * part, (half + 1) * part)
            _, d_gate_pre, d_up_pre = hidden_back(
                d_hiddens[i][:, at], gp_ref[half, span, cols], upre_ref[half, span, cols], None
            )
            dg_ref[x ^ half, span, cols] = d_gate_pre
            du_ref[x ^ half, span, cols] = d_up_pre
            term = mm_nt(d_gate_pre, s_gate[:, at]) + mm_nt(d_up_pre, s_up[:, at])
            total = term if total is None else total + term
        acc_ref[span] = total
    sent = []
    for e in range(here):
        expert = info_ref[0] * here + e
        half, at = e // 2, (e % 2) * width
        cols = slice(at, at + width)
        for i, span in enumerate(spans):
            d_gate, d_gate_pre, d_up_pre = hidden_back(
                mm(g_ref[span], down_ref[e]),
                gp_ref[half, span, cols],
                upre_ref[half, span, cols],
                gate_column(extras[i], lane, expert),
            )
            dg_ref[x ^ half, span, cols] = d_gate_pre
            du_ref[x ^ half, span, cols] = d_up_pre
            d_gates[i] = jnp.where(lane == expert, d_gate, d_gates[i])
            acc_ref[span] += mm_nt(d_gate_pre, gate_ref[e]) + mm_nt(d_up_pre, up_ref[e])
        if e + 1 == here:
            sent = [
                start_copy(dg_ref.at[0], dg_out, sems, 16),
                start_copy(du_ref.at[0], du_out, sems, 17),
            ]
    for i, ref in enumerate((dxa_ref, dxb_ref, dxc_ref, dxd_ref)):
        at = slice(i * rows, (i + 1) * rows)
        own = slice(i % 2 * rows, (i % 2 + 1) * rows)
        extra = split_low(d_gates[i // 2], lane, 16)[own]
        ref[:, :features] = acc_ref[at].astype(ref.dtype)
        ref[:, features:] = extra.astype(ref.dtype)
    sent.append(start_copy(dxa_ref, dxa_hbm, sems, 18))
    wait_all(sent)


def experts_back_call(info, grads, exts, kept, weights):
    rows, features = grads[0].shape[0], grads[0].shape[1] - EXTRA
    _, held, wide = kept[0].shape
    ext = grads[0].shape
    return pl.pallas_call(
        experts_back_kernel,
        out_shape=(
            hbm(ext, f32),
            jax.ShapeDtypeStruct(ext, bf16),
            jax.ShapeDtypeStruct(ext, f32),
            jax.ShapeDtypeStruct(ext, bf16),
        )
        + (hbm((2 * held, wide), bf16),) * 2,
        in_specs=[in_smem] + [in_vmem] * 4 + [anywhere] * 12,
        out_specs=(anywhere,) + (in_vmem,) * 3 + (anywhere,) * 2,
        scratch_shapes=[pltpu.VMEM((2, 2 * held, wide), bf16)] * 4
        + [
            pltpu.VMEM((4 * rows, features), bf16),
            pltpu.VMEM((4 * rows, EXTRA), bf16),
            pltpu.VMEM(ext, f32),
            pltpu.VMEM((4 * rows, features), f32),
            pltpu.SemaphoreType.DMA((19,)),
        ],
        compiler_params=limits(24),
        cost_estimate=cost(24),
        name="experts_backward",
    )(info, *weights, *[in_hbm(value) for value in (*grads, *exts, *kept)])


def pair_shared(info_ref, shared_ref, which):
    width = shared_ref.shape[1] // 3
    first = which * width + info_ref[1] * (width // 2)
    return shared_ref[:, pl.ds(pl.multiple_of(first, 128), width // 2)]


def pair_kernel(info_ref, gate_ref, up_ref, shared_ref, x0, x1, x2, x3,
                gp_out, upre_out, hid_out, gp_ref, upre_ref, hid_ref, x_ref, extra_ref, sems):
    here, _, width = gate_ref.shape
    count = here // 2
    wait_all(load_rows((x0, x1, x2, x3), x_ref, extra_ref, sems, 3))
    extra = extra_ref[...].astype(f32)
    lane = lanes_of(extra.shape[0])
    for j in range(count + 1):
        if j < count:
            gate_w, up_w = gate_ref[info_ref[1] * count + j], up_ref[info_ref[1] * count + j]
        else:
            gate_w, up_w = (pair_shared(info_ref, shared_ref, i) for i in range(2))
        gate_pre, up_pre = mm(x_ref[...], gate_w), mm(x_ref[...], up_w)
        hidden = gate_pre * jax.nn.sigmoid(gate_pre) * up_pre
        if j < count:
            expert = info_ref[0] * here + info_ref[1] * count + j
            hidden = hidden * gate_column(extra, lane, expert)
        cols = slice(j * width, j * width + gate_pre.shape[1])
        gp_ref[:, cols] = gate_pre.astype(bf16)
        upre_ref[:, cols] = up_pre.astype(bf16)
        hid_ref[:, cols] = hidden.astype(bf16)
    wait_all(
        [
            start_copy(source, target, sems, i)
            for i, (source, target) in enumerate(
                [(hid_ref, hid_out), (gp_ref, gp_out), (upre_ref, upre_out)]
            )
        ]
    )


def pair_call(info, exts, weights):
    rows, features = 4 * exts[0].shape[0], exts[0].shape[1] - EXTRA
    e_gate, e_up, _, shared = weights
    wide = (rows, e_gate.shape[0] // 2 * e_gate.shape[2] + shared.shape[1] // 6)
    return pl.pallas_call(
        pair_kernel,
        out_shape=(hbm(wide, bf16),) * 3,
        in_specs=[in_smem] + [in_vmem] * 3 + [anywhere] * 4,
        out_specs=(anywhere,) * 3,
        scratch_shapes=[pltpu.VMEM(wide, bf16)] * 3
        + [
            pltpu.VMEM((rows, features), bf16),
            pltpu.VMEM((rows, EXTRA), bf16),
            pltpu.SemaphoreType.DMA((11,)),
        ],
        compiler_params=limits(16),
        cost_estimate=cost(8),
        name="pair_forward",
    )(info, e_gate, e_up, shared, *[in_hbm(value) for value in exts])


def pair_back_kernel(info_ref, down_ref, shared_ref, g0, g1, g2, g3, e0, e1, e2, e3, gp_in, upre_in,
                     dg_out, du_out, gp_ref, upre_ref, dg_ref, du_ref, g_ref, extra_ref, sems):
    rows, features = g0.shape[0], g_ref.shape[1]
    here, _, width = down_ref.shape
    count = here // 2
    loads = load_rows((g0, g1, g2, g3), g_ref, None, sems, 4)
    loads += [start_copy(gp_in, gp_ref, sems, 0), start_copy(upre_in, upre_ref, sems, 1)]
    for i, source in enumerate((e0, e1, e2, e3)):
        lanes = source.at[:, pl.ds(features, EXTRA)]
        loads.append(start_copy(lanes, extra_ref.at[pl.ds(i * rows, rows)], sems, 12 + i))
    wait_all(loads)
    extra = extra_ref[...].astype(f32)
    lane = lanes_of(4 * rows)
    for j in range(count + 1):
        gate = None
        if j < count:
            weight = down_ref[info_ref[1] * count + j]
            gate = gate_column(extra, lane, info_ref[0] * here + info_ref[1] * count + j)
        else:
            weight = pair_shared(info_ref, shared_ref, 2)
        cols = slice(j * width, j * width + weight.shape[1])
        _, d_gate_pre, d_up_pre = hidden_back(
            mm(g_ref[...], weight), gp_ref[:, cols], upre_ref[:, cols], gate
        )
        dg_ref[:, cols] = d_gate_pre
        du_ref[:, cols] = d_up_pre
    wait_all([start_copy(dg_ref, dg_out, sems, 2), start_copy(du_ref, du_out, sems, 3)])


def pair_back_call(info, grads, exts, gate_pre, up_pre, weights):
    rows, features = 4 * exts[0].shape[0], exts[0].shape[1] - EXTRA
    wide = gate_pre.shape
    return pl.pallas_call(
        pair_back_kernel,
        out_shape=(hbm(wide, bf16),) * 2,
        in_specs=[in_smem] + [in_vmem] * 2 + [anywhere] * 10,
        out_specs=(anywhere,) * 2,
        scratch_shapes=[pltpu.VMEM(wide, bf16)] * 4
        + [
            pltpu.VMEM((rows, features), bf16),
            pltpu.VMEM((rows, EXTRA), bf16),
            pltpu.SemaphoreType.DMA((16,)),
        ],
        compiler_params=limits(16),
        cost_estimate=cost(7),
        name="pair_backward",
    )(info, weights[2], weights[3], *[in_hbm(value) for value in (*grads, *exts, gate_pre, up_pre)])


def weight_grad_kernel(*refs):
    lefts, rights, (out_ref, left_ref, right_ref, tiles_ref, sems) = refs[:8], refs[8:-5], refs[-5:]
    features = left_ref.shape[1]
    loads, at = load_rows(lefts, left_ref, None, sems, 3), 0
    for i, ref in enumerate(rights):
        target = right_ref.at[pl.ds(at, ref.shape[0])]
        loads.append(start_copy(ref, target, sems, 19 + i))
        at += ref.shape[0]
    wait_all(loads)
    rows = left_ref.shape[0]
    tile, wide = tiles_ref.shape[1:]
    sent = []
    for group in range(right_ref.shape[0] // rows):
        right = slice(group * rows, (group + 1) * rows)
        for t in range(features // tile):
            cols = slice(t * tile, (t + 1) * tile)
            index = group * (features // tile) + t
            slot = index % tiles_ref.shape[0]
            if len(sent) >= tiles_ref.shape[0]:
                sent[index - tiles_ref.shape[0]].wait()
            tiles_ref[slot] = mm_tn(left_ref[:, cols], right_ref[right]).astype(bf16)
            target = out_ref.at[pl.ds(t * tile, tile), pl.ds(group * wide, wide)]
            sent.append(start_copy(tiles_ref.at[slot], target, sems, slot))
    wait_all(sent[-tiles_ref.shape[0] :])


def weight_grad_call(lefts, rights):
    rows = sum(value.shape[0] for value in lefts)
    features, wide = lefts[0].shape[1] - EXTRA, rights[0].shape[1]
    held = sum(value.shape[0] for value in rights)
    operands = [in_hbm(value) for value in (*lefts, *rights)]
    return pl.pallas_call(
        weight_grad_kernel,
        out_shape=hbm((features, held // rows * wide), bf16),
        in_specs=[anywhere] * len(operands),
        out_specs=anywhere,
        scratch_shapes=[
            pltpu.VMEM((rows, features), bf16),
            pltpu.VMEM((held, wide), bf16),
            pltpu.VMEM((3, 256, wide), bf16),
            pltpu.SemaphoreType.DMA((19 + len(rights),)),
        ],
        compiler_params=limits(16),
        cost_estimate=cost(8 * held // rows),
        name="weight_gradients",
    )(*operands)


def exchange_wa(pick):
    return [pick(0)] + [swap(pick(i), "wa", i) for i in (1, 2, 3)]


def after(values, *done):
    kept = lax.optimization_barrier((values, done))
    return kept[0]


def key_blocks(kv, n):
    levels = [kv]
    for s in range(1, n // 2):
        levels.append(lax.ppermute(kv, "ctx", [(i, i + 2 * s) for i in range(n - 2 * s)]))
    blocks = []
    for level in levels:
        blocks += [level, swap(level, "ctx", 1)]
    return blocks


def sum_key_blocks(own, moved, n, beside):
    m, rows = n // 2, own[0].shape[0]
    got = [both[i : i + rows] for both in moved for i in range(0, both.shape[0], rows)]
    total, beside = None, list(beside)
    for s in reversed(range(m)):
        level = own[s].astype(f32) + got[s].astype(f32)
        if s:
            level = lax.ppermute(
                level.astype(bf16), "ctx", [(i + 2 * s, i) for i in range(n - 2 * s)]
            )
            if beside:
                level = after(level, beside.pop(0))
            level = level.astype(f32)
        total = level if total is None else total + level
    return total.astype(bf16)


def sum_pairs(value, n):
    groups = [[2 * i + x for i in range(n // 2)] for x in range(2)]
    return lax.psum_scatter(
        value, "ctx", scatter_dimension=0, tiled=True, axis_index_groups=groups
    )


def per_device(
    tokens,
    teacher,
    lengths,
    routes,
    query_weight,
    key_projection_matrix,
    value_projection_matrix,
    output_weight,
    attn_gain,
    moe_gain,
    router_weight,
    shared_gate,
    shared_up,
    shared_down,
    expert_gate,
    expert_up,
    expert_down,
):
    w = lax.axis_index("wa")
    c = lax.axis_index("ctx")
    n = lax.axis_size("ctx")
    groups = lax.axis_size("wa")
    x, z, m = c % 2, c // 2, n // 2
    own_tokens = tokens[0]
    rows, features = own_tokens.shape
    slab = features // groups
    experts_all = router_weight.shape[1]
    length = jnp.sum(jnp.where(jnp.arange(lengths.shape[0]) == w, lengths, 0))
    count = jnp.sum(lengths).astype(f32)
    qpos = c * rows + jnp.arange(rows)
    width = KEY_VALUE_HEADS * HEAD_SIZE
    z_low = z % 2
    w_info = jnp.stack([w, x, z_low]).astype(jnp.int32)

    def columns(value, index):
        return lax.dynamic_slice_in_dim(value, index * slab, slab, 1)

    input_rows = own_tokens.astype(f32)
    factor_a = rms_factor(input_rows)
    far_half = lax.dynamic_slice_in_dim(own_tokens, (1 - w // 2) * 2 * slab, 2 * slab, 1)
    far_tokens = swap(far_half, "wa", 2)
    far_factor = swap(factor_a, "wa", 2)
    small = jnp.concatenate([router_weight.T, attn_gain[None], moe_gain[None]], axis=0)
    near_small = swap(small, "wa", 1)
    far_small = swap(small, "wa", 2)
    own_weights = (key_projection_matrix, value_projection_matrix, query_weight)
    near_weights = tuple(swap(value, "wa", 1) for value in own_weights)

    gain_own = small[-2:-1].astype(f32)
    gain_near = near_small[-2:-1].astype(f32)
    core = w % 2

    def far_columns(index):
        return lax.dynamic_slice_in_dim(far_tokens, index * slab, slab, 1)

    part_own = jnp.concatenate([columns(own_tokens, w), far_columns(core)], axis=0)
    part_near = jnp.concatenate([columns(own_tokens, w ^ 1), far_columns(1 - core)], axis=0)
    both_factor = jnp.concatenate([factor_a, far_factor], axis=0)
    normed_own = (part_own.astype(f32) * both_factor * gain_own).astype(bf16)
    normed_near = (part_near.astype(f32) * both_factor * gain_near).astype(bf16)

    def project(i):
        return mm(normed_own, own_weights[i]) + mm(normed_near, near_weights[i])

    kv_terms = jnp.concatenate([project(0), project(1)], axis=1)
    kv_got = swap(after(kv_terms[rows:].astype(bf16), far_small), "wa", 2)
    kv = (kv_terms[:rows] + kv_got.astype(f32)).astype(bf16)
    q_terms = project(2)

    half_out = output_weight.shape[1] // 2
    half_weight = lax.dynamic_slice_in_dim(output_weight, z_low * half_out, half_out, 1)
    q_got = swap(after(q_terms[rows:].astype(bf16), kv_got), "wa", 2)
    query_rows = (q_terms[:rows] + q_got.astype(f32)).astype(bf16)
    far_out = swap(after(half_weight, kv_got), "wa", 2)
    if n > 8:
        first_keys, all_keys = [], []
    else:
        kv_all = key_blocks(kv, n)
        first_keys, all_keys = [kv_all[1]] + kv_all[2::2], kv_all[1:]

    shared_width = shared_gate.shape[1] // groups

    shared_weights = after((shared_gate, shared_up, shared_down), kv_got)

    def shared_chunk(i):
        return jnp.concatenate(
            [
                lax.dynamic_slice_in_dim(value, (w ^ i) * shared_width, shared_width, 1)
                for value in shared_weights
            ],
            axis=1,
        )

    shared_far = swap(
        after(jnp.concatenate([shared_chunk(2), shared_chunk(3)]), far_out, q_got, *first_keys), "wa", 2
    )
    far_pair = jnp.concatenate([far_out, swap(far_out, "ctx", 2)])
    output_parts = [
        output_weight,
        swap(output_weight, "wa", 1),
        far_pair,
        swap(after(far_pair, *all_keys), "wa", 1),
    ]
    smalls = jnp.concatenate(
        perm4([small, near_small, far_small, swap(far_small, "wa", 1)], w), axis=1
    )
    router_t = jnp.pad(smalls[:experts_all], ((0, EXTRA - experts_all), (0, 0)))
    gain_a, gain_b = smalls[-2:-1].astype(f32), smalls[-1:].astype(f32)

    if n > 8:
        kv_all, pos = gather_keys(kv, c, n)
        q = heads(query_rows, GROUP)
        attn, kept_attn = attention_forward(q, kv_all, pos, qpos, length)
        attn = attn.reshape(rows, -1)
        attn_out = attn.astype(bf16)
    else:
        first = [c, length]
        for s in range(m):
            first += [(c - 2 * s) * rows, (c - 2 * s + 1 - 2 * x) * rows]
        attn_out, attn, kept_attn = attention_call(
            jnp.stack(first).astype(jnp.int32), query_rows, kv_all
        )
    resid, row_ext, gates = branch_call(
        w_info, attn_out, output_parts, own_tokens, gain_b, router_t, routes[0]
    )
    shared_parts = [
        shared_chunk(0),
        swap(shared_chunk(1), "wa", 1),
        shared_far[:slab],
        swap(after(shared_far[slab:], attn_out), "wa", 1),
    ]
    shared_mine = jnp.concatenate(perm4(shared_parts, w))
    weights = (expert_gate, expert_up, expert_down, shared_mine)

    row_parts = [row_ext, swap(row_ext, "wa", 1), swap(row_ext, "wa", 2)]
    rows_own = swap(row_ext, "ctx", 1)
    done = [experts_call(w_info, row_parts[0], row_parts[1], weights)]
    row_parts[2] = after(row_parts[2], done[0][1], rows_own)
    row_parts.append(swap(row_parts[2], "wa", 1))
    rows_far = swap(row_parts[2], "ctx", 1)
    rows_pair = row_parts + [rows_own, swap(rows_own, "wa", 1), rows_far, swap(rows_far, "wa", 1)]
    done.append(experts_call(w_info, row_parts[2], row_parts[3], weights))

    def sum_wa(own, near, far, far_near):
        far = far + swap(far_near, "wa", 1).astype(f32)
        return own, swap(near, "wa", 1), far.astype(bf16)

    own_out, near_out, far_out = sum_wa(done[0][0], done[0][1], done[1][0], done[1][1])
    far_out = after(swap(far_out, "wa", 2), rows_far)
    gate_pre_pair, up_pre_pair, hidden_pair = pair_call(w_info, rows_pair[4:], weights)
    scale = lengths.shape[0] * n * rows / count
    block_out, grad_result, grad_ext = result_call(
        jnp.stack([c, length]).astype(jnp.int32), scale[None], resid, own_out, near_out, far_out, teacher[0]
    )
    grad_parts = [grad_ext, swap(grad_ext, "wa", 1), swap(grad_ext, "wa", 2)]
    pair_own = swap(grad_ext, "ctx", 1)

    grad_parts[2], pair_own = after((grad_parts[2], pair_own), hidden_pair)
    grad_parts.append(swap(grad_parts[2], "wa", 1))
    pair_far = swap(grad_parts[2], "ctx", 1)
    grads_pair = grad_parts + [pair_own, swap(pair_own, "wa", 1), pair_far, swap(pair_far, "wa", 1)]
    down_terms = weight_grad_call(grads_pair, [done[0][4], done[1][4], hidden_pair])
    down_sum = sum_pairs(down_terms, n)

    kept = (done[0][2], done[1][2], done[0][3], done[1][3])
    first_grad = after(grad_parts[0], down_terms)
    back = experts_back_call(w_info, [first_grad] + grad_parts[1:], row_parts, kept, weights)
    own_back, near_back, far_back = sum_wa(*back[:4])
    grads_pair[4] = after(grads_pair[4], far_back)
    far_back = swap(far_back, "wa", 2)
    gate_pair, up_pair = pair_back_call(
        w_info, grads_pair[4:], rows_pair[4:], gate_pre_pair, up_pre_pair, weights
    )
    gate_pair = after(gate_pair, far_back)
    pre_terms = weight_grad_call(rows_pair, [back[4], gate_pair, back[5], up_pair])
    far_back = after(far_back, pre_terms)
    grad_resid, gz, d_attn, small_b = resid_back_call(
        w_info, own_back, near_back, far_back, grad_result, resid, row_ext, gates, gain_b,
        router_t, output_parts, experts_all,
    )

    fine_rows = features // n

    def whole_rows(summed):
        ours = lax.dynamic_slice_in_dim(summed, x * fine_rows, fine_rows, 0)
        got = swap(lax.dynamic_slice_in_dim(summed, (1 - x) * fine_rows, fine_rows, 0), "ctx", 1)
        return jnp.where(x == 0, ours, got), jnp.where(x == 0, got, ours)

    fine = features // n // groups

    def fine_exchange(value):
        blocks = jnp.transpose(value.reshape(-1, n, groups, fine), (2, 0, 1, 3))
        blocks = blocks.reshape(groups, -1, slab)
        return exchange_wa(lambda i: lax.dynamic_index_in_dim(blocks, w ^ i, 0, keepdims=False))

    attn_in = (input_rows * factor_a * gain_a).astype(bf16)
    attn_in_fine = jnp.concatenate(fine_exchange(attn_in))
    gz_fine = jnp.concatenate(fine_exchange(gz))

    def fold_rows(value):
        blocks = value.astype(bf16).reshape(m, 2, fine, value.shape[1])
        mine = lax.dynamic_index_in_dim(blocks, x, 1, keepdims=False)
        got = swap(lax.dynamic_index_in_dim(blocks, 1 - x, 1, keepdims=False), "ctx", 1)
        summed = (mine.astype(f32) + got.astype(f32)).astype(bf16)
        return summed.reshape(m * fine, -1)


    if n > 8:
        d_heads = heads(d_attn, GROUP)
        delta = jnp.sum(d_heads.astype(f32) * heads(attn, GROUP), axis=-1)
        delta = jnp.transpose(delta, (1, 2, 0))[..., None]
        d_q, d_kv = attention_backward(q, kv_all, pos, qpos, length, kept_attn, d_heads, delta)
        d_q = d_q.reshape(rows, -1).astype(bf16)
        d_kv, moved = scatter_keys(d_kv, n).astype(bf16), []
    else:
        d_q, d_own, d_pair = attention_back_call(d_attn, query_rows, attn, kept_attn, kv_all)
        moved = [swap(jnp.concatenate(d_pair[at : at + 2]), "ctx", 1) for at in range(0, m, 2)]
    attn_parts = gather_wa(after(attn_out, d_q))
    grad_output = fold_rows(mm_tn(gz_fine, jnp.concatenate(attn_parts)))
    d_q_parts = gather_wa(after(d_q, *moved))
    grad_query = fold_rows(mm_tn(attn_in_fine, jnp.concatenate(d_q_parts)))
    down_halves = whole_rows(after(down_sum, d_q))
    if n <= 8:
        d_kv = sum_key_blocks(d_own, moved, n, (grad_output, grad_query, down_halves[0]))
    pre_sum = sum_pairs(after(pre_terms, down_sum, d_q), n)
    d_kv_parts = gather_wa(d_kv)

    both_d_q = jnp.concatenate([d_q, d_q_parts[2]])
    both_d_kv = jnp.concatenate([d_kv, d_kv_parts[2]])

    def back_through(weights):
        both = (both_d_kv[:, :width], both_d_kv[:, width:], both_d_q)
        return sum(mm_nt(value, weight) for value, weight in zip(both, weights, strict=True))

    back_own, back_near = back_through(own_weights), back_through(near_weights)
    returned = swap(
        jnp.concatenate([back_own[rows:], back_near[rows:]], axis=1).astype(bf16), "wa", 2
    ).astype(f32)
    grad_attn_in = jnp.concatenate(
        perm4([back_own[:rows], back_near[:rows], returned[:, :slab], returned[:, slab:]], w),
        axis=1,
    )
    grad_norm_a, grad_gain_a = norm_backward(input_rows, factor_a, gain_a, grad_attn_in)
    grad_tokens = grad_resid + grad_norm_a

    grad_kv = fold_rows(mm_tn(attn_in_fine, jnp.concatenate(d_kv_parts)))
    dense_terms = jnp.concatenate([grad_output, grad_query, grad_kv], axis=1)

    loss_part = jnp.sum(grad_ext[:, features:].astype(f32))
    smalls_grad = jnp.concatenate(
        [small_b[: experts_all + 1], grad_gain_a[None], jnp.full((1, features), loss_part)], axis=0
    )
    parts = fine_exchange(smalls_grad)
    small_sum = (parts[0] + parts[1] + parts[2] + parts[3]).reshape(-1, n, fine)
    small_sum = after(jnp.transpose(small_sum, (1, 0, 2)), dense_terms)
    if m == 4:
        blocks = small_sum.reshape((m, 2) + small_sum.shape[1:])
        got = swap(lax.dynamic_index_in_dim(blocks, 1 - x, 1, keepdims=False), "ctx", 1)
        blocks = lax.dynamic_index_in_dim(blocks, x, 1, keepdims=False) + got
        parts = [lax.dynamic_index_in_dim(blocks, z ^ i, 0, keepdims=False) for i in range(m)]
        small_sum = parts[0] + sum(swap(parts[i], "ctx", 2 * i) for i in range(1, m))
    else:
        small_sum = lax.all_to_all(small_sum, "ctx", split_axis=0, concat_axis=0, tiled=True)
        small_sum = jnp.sum(small_sum, axis=0)
    loss = small_sum[-1, 0] / (2.0 * features * count)
    dense = sum_pairs(after(dense_terms, pre_sum, small_sum), n).astype(f32)
    pieces, at = [], 0
    for size in (output_weight.shape[1], query_weight.shape[1], width, width):
        pieces.append(dense[:, at : at + size])
        at += size

    units = expert_gate.shape[2]
    used = expert_gate.shape[0] // 2 * units

    def experts_of(first, second, at):
        return jnp.stack(
            [
                value[:, at + e * units : at + (e + 1) * units].astype(f32)
                for value in (first, second)
                for e in range(expert_gate.shape[0] // 2)
            ]
        )

    wide = down_sum.shape[1]
    pre_halves = whole_rows(after(pre_sum, dense_terms))
    grad_expert_down = experts_of(*down_halves, 0)
    grad_expert_gate = experts_of(*pre_halves, 0)
    grad_expert_up = experts_of(*pre_halves, wide)
    shared = jnp.concatenate(
        [value[:, used:] for value in down_halves]
        + [value[:, used:wide] for value in pre_halves]
        + [value[:, wide + used :] for value in pre_halves],
        axis=1,
    )

    def shared_rows(i):
        return lax.dynamic_slice_in_dim(shared, (w ^ i) * fine, fine, 0)

    shared = jnp.stack(perm4(exchange_wa(shared_rows), w)).astype(f32)
    shared = shared.reshape(groups, fine, 3, shared_width)
    grad_shared_down, grad_shared_gate, grad_shared_up = (
        jnp.transpose(shared[:, :, i], (1, 0, 2)).reshape(fine, -1) for i in range(3)
    )

    return (
        block_out[None],
        grad_tokens[None],
        pieces[1],
        pieces[2],
        pieces[3],
        pieces[0],
        small_sum[experts_all + 1],
        small_sum[experts_all],
        small_sum[:experts_all].T,
        grad_shared_gate,
        grad_shared_up,
        grad_shared_down,
        grad_expert_gate,
        grad_expert_up,
        grad_expert_down,
        loss,
    )


def solution(mesh):
    return jax.shard_map(
        per_device,
        mesh=mesh,
        in_specs=(
            P("wa", "ctx", None),
            P("wa", "ctx", None),
            P(),
            P("wa", "ctx", None),
            P("wa", None),
            P("wa", None),
            P("wa", None),
            P("wa", None),
            P("wa"),
            P("wa"),
            P("wa", None),
            P("wa", None),
            P("wa", None),
            P("wa", None),
            P("wa", None, None),
            P("wa", None, None),
            P("wa", None, None),
        ),
        out_specs=(
            P("wa", "ctx", None),
            P("wa", "ctx", None),
            P(("ctx", "wa"), None),
            P(("ctx", "wa"), None),
            P(("ctx", "wa"), None),
            P(("ctx", "wa"), None),
            P(("ctx", "wa")),
            P(("ctx", "wa")),
            P(("ctx", "wa"), None),
            P(("ctx", "wa"), None),
            P(("ctx", "wa"), None),
            P(("ctx", "wa"), None),
            P("wa", "ctx", None),
            P("wa", "ctx", None),
            P("wa", "ctx", None),
            P(),
        ),
        check_vma=False,
    )
```

profile of v0, /device:TPU:0, one launch (start us, length us, event | category | flops | bytes accessed | tf_op | source)
XLA Modules:
  0.0 451.1 jit_solution(15401105794724476042)
XLA Ops:
  10.0 2.6 collective-permute-start.6
  15.5 2.0 collective-permute-start.1
  28.7 7.9 %collective-permute-done.7 = bf16[128,1024]{1,0:T(8,128)(2,1)S(1)} collective-permute-done((bf16[128,1024]{1,0:T(8,128)(2,1)S(1)}, bf16[128,1024]{1,0:T(8,128)(2,1)S(1)}, u32[]{:S(2)}, u32[]{:S(2)}) %collective-permute-start.7) | collective-permute-done | bytes 262176 | tf_op jit(solution)/shard_map/ppermute | solution.py:38
  37.6 3.7 collective-permute-start.10
  41.3 4.5 collective-permute-start.12
  55.7 2.9 collective-permute-done.14.refs_6_
  60.7 2.0 collective-permute-done.8
  63.3 6.7 %collective-permute-done.18 = bf16[384,768]{1,0:T(8,128)(2,1)S(1)} collective-permute-done((bf16[384,768]{1,0:T(8,128)(2,1)S(1)}, bf16[384,768]{1,0:T(8,128)(2,1)S(1)}, u32[]{:S(2)}, u32[]{:S(2)}) %collective-permute-start.18) | collective-permute-done | bytes 589856 | tf_op jit(solution)/shard_map/ppermute | solution.py:38
  72.0 5.8 %attention_forward.1 = (bf16[128,1536]{1,0:T(8,128)(2,1)}, f32[128,1536]{1,0:T(8,128)}, bf16[4,8,384,128]{3,2,1,0:T(8,128)(2,1)}) custom-call(s32[10]{0:T(128)S(1)} %stack.146.info_ref, bf16[128,1536]{1,0:T(8,128)(2,1)S(1)} %fusion.32.q_ref.q_in, bf16[128,1024]{1,0:T(8,128)(2,1)S(1)} %fusion.39.refs_0_, ...), custom_call_target="tpu_custom_call" | custom-call | flops 5750000128 | tf_op jit(solution)/shard_map/attention_forward/pallas_call | solution.py:313
  77.9 9.9 %collective-permute-done.22 = bf16[768,768]{1,0:T(8,128)(2,1)S(1)} collective-permute-done((bf16[768,768]{1,0:T(8,128)(2,1)S(1)}, bf16[768,768]{1,0:T(8,128)(2,1)S(1)}, u32[]{:S(2)}, u32[]{:S(2)}) %collective-permute-start.22) | collective-permute-done | bytes 1179680 | tf_op jit(solution)/shard_map/ppermute | solution.py:38
  88.2 4.8 %branch_and_router.1 = (f32[128,1536]{1,0:T(8,128)}, bf16[128,1664]{1,0:T(8,128)(2,1)S(1)}, f32[128,128]{1,0:T(8,128)S(1)}) custom-call(s32[3]{0:T(128)S(1)} %pad_add_fusion.1.info_ref, bf16[128,1536]{1,0:T(8,128)(2,1)} %get-tuple-element.140.attn_ref, bf16[384,1536]{1,0:T(8,128)(2,1)S(1)} %copy-done.3, ...), custom_call_target="tpu_custom_call" | custom-call | flops 5175000064 | tf_op jit(solution)/shard_map/branch_and_router/pallas_call | solution.py:444
  98.2 8.2 %experts_forward.2 = (f32[128,1536]{1,0:T(8,128)}, bf16[128,1536]{1,0:T(8,128)(2,1)S(1)}, bf16[2,256,1152]{2,1,0:T(8,128)(2,1)}, bf16[2,256,1152]{2,1,0:T(8,128)(2,1)}, bf16[256,1152]{1,0:T(8,128)(2,1)}) custom-call(s32[3]{0:T(128)S(1)} %pad_add_fusion.1.info_ref, bf16[128,1664]{1,0:T(8,128)(2,1)S(1)} %get-tuple-element.92.xa_ref.refs_8_.refs_0_.refs_4_, ...), custom_call_target="tpu_custom_call" | custom-call | flops 9200000000 | tf_op jit(solution)/shard_map/experts_forward/pallas_call | solution.py:644
  108.3 7.7 %experts_forward.3 = (f32[128,1536]{1,0:T(8,128)}, bf16[128,1536]{1,0:T(8,128)(2,1)S(1)}, bf16[2,256,1152]{2,1,0:T(8,128)(2,1)}, bf16[2,256,1152]{2,1,0:T(8,128)(2,1)}, bf16[256,1152]{1,0:T(8,128)(2,1)}) custom-call(s32[3]{0:T(128)S(1)} %pad_add_fusion.1.info_ref, bf16[128,1664]{1,0:T(8,128)(2,1)S(1)} %collective-permute-done.26.xa_ref.refs_10_.refs_2_, ...), custom_call_target="tpu_custom_call" | custom-call | flops 9200000000 | tf_op jit(solution)/shard_map/experts_forward/pallas_call | solution.py:644
  121.8 6.6 %collective-permute-done.31.x2.e2.refs_6_ = bf16[128,1664]{1,0:T(8,128)(2,1)} collective-permute-done((bf16[128,1664]{1,0:T(8,128)(2,1)S(1)}, bf16[128,1664]{1,0:T(8,128)(2,1)}, u32[]{:S(2)}, u32[]{:S(2)}) %collective-permute-start.31) | collective-permute-done | bytes 426016 | tf_op jit(solution)/shard_map/ppermute | solution.py:38
  131.3 4.2 result_and_error.1
  137.6 2.8 copy-done.8
  140.4 2.8 copy-done.10
  143.2 8.1 %pair_forward.1 = (bf16[512,1152]{1,0:T(8,128)(2,1)}, bf16[512,1152]{1,0:T(8,128)(2,1)}, bf16[512,1152]{1,0:T(8,128)(2,1)}) custom-call(s32[3]{0:T(128)S(1)} %pad_add_fusion.1.info_ref, bf16[4,1536,512]{2,1,0:T(8,128)(2,1)S(1)} %copy-done.8, bf16[4,1536,512]{2,1,0:T(8,128)(2,1)S(1)} %copy-done.10, bf16[1536,768]{1,0:T(8,128)(2,1)S(1)} %pad_maximum_fusion.shared_ref.refs_3_, ...), custom_call_target="tpu_custom_call" | custom-call | flops 9200000000 | tf_op jit(solution)/shard_map/pair_forward/pallas_call | solution.py:826
  153.4 8.5 %collective-permute-done.39.refs_6_.g2 = bf16[128,1664]{1,0:T(8,128)(2,1)S(1)} collective-permute-done((bf16[128,1664]{1,0:T(8,128)(2,1)S(1)}, bf16[128,1664]{1,0:T(8,128)(2,1)S(1)}, u32[]{:S(2)}, u32[]{:S(2)}) %collective-permute-start.39) | collective-permute-done | bytes 426016 | tf_op jit(solution)/shard_map/ppermute | solution.py:38
  164.5 8.7 %weight_gradients.2 = bf16[1536,1152]{1,0:T(8,128)(2,1)} custom-call(bf16[128,1664]{1,0:T(8,128)(2,1)} %copy-done.7, bf16[128,1664]{1,0:T(8,128)(2,1)} %copy-done.77, bf16[128,1664]{1,0:T(8,128)(2,1)} %copy-done.74, bf16[128,1664]{1,0:T(8,128)(2,1)} %copy-done.78, bf16[128,1664]{1,0:T(8,128)(2,1)} %copy-done.72, bf16[128,1664]{1,0:T(8,128)(2,1)} %copy-done.75, ...), custom_call_target="tpu_custom_call" | custom-call | flops 9200000000 | tf_op jit(solution)/shard_map/weight_gradients/pallas_call | solution.py:923
  173.2 2.8 copy-done.9
  176.0 2.8 copy-done.11
  178.8 2.8 copy-done.12
  181.6 20.2 %experts_backward.1 = (f32[128,1664]{1,0:T(8,128)}, bf16[128,1664]{1,0:T(8,128)(2,1)}, f32[128,1664]{1,0:T(8,128)S(1)}, bf16[128,1664]{1,0:T(8,128)(2,1)S(1)}, b...) custom-call(s32[3]{0:T(128)S(1)} %pad_add_fusion.1.info_ref, bf16[4,1536,512]{2,1,0:T(8,128)(2,1)S(1)} %copy-done.9, ...), custom_call_target="tpu_custom_call" | custom-call | flops 27599998976 | tf_op jit(solution)/shard_map/experts_backward/pallas_call | solution.py:760
  203.8 7.0 %pair_backward.1 = (bf16[512,1152]{1,0:T(8,128)(2,1)}, bf16[512,1152]{1,0:T(8,128)(2,1)}) custom-call(s32[3]{0:T(128)S(1)} %pad_add_fusion.1.info_ref, bf16[4,1536,512]{2,1,0:T(8,128)(2,1)S(1)} %copy-done.12, bf16[1536,768]{1,0:T(8,128)(2,1)S(1)} %pad_maximum_fusion.shared_ref.refs_3_, bf16[128,1664]{1,0:T(8,128)(2,1)} %copy-done.72, ...), custom_call_target="tpu_custom_call" | custom-call | flops 8049999872 | tf_op jit(solution)/shard_map/pair_backward/pallas_call | solution.py:875
  210.8 4.8 %collective-permute-done.42.far_ref = bf16[128,1664]{1,0:T(8,128)(2,1)S(1)} collective-permute-done((bf16[128,1664]{1,0:T(8,128)(2,1)S(1)}, bf16[128,1664]{1,0:T(8,128)(2,1)S(1)}, u32[]{:S(2)}, u32[]{:S(2)}) %collective-permute-start.42) | collective-permute-done | bytes 426016 | tf_op jit(solution)/shard_map/ppermute | solution.py:38
  216.4 14.6 %weight_gradients.3 = bf16[1536,2304]{1,0:T(8,128)(2,1)} custom-call(bf16[128,1664]{1,0:T(8,128)(2,1)} %copy-done.15, bf16[128,1664]{1,0:T(8,128)(2,1)} %copy-done.16, bf16[128,1664]{1,0:T(8,128)(2,1)} %copy-done.17, bf16[128,1664]{1,0:T(8,128)(2,1)} %copy-done.18, bf16[128,1664]{1,0:T(8,128)(2,1)} %collective-permute-done.27.x0.e0.refs_4_, ...), custom_call_target="tpu_custom_call" | custom-call | flops 18400000000 | tf_op jit(solution)/shard_map/weight_gradients/pallas_call | solution.py:923
  231.0 5.1 %residual_backward.1 = (f32[128,1536]{1,0:T(8,128)}, bf16[128,1536]{1,0:T(8,128)(2,1)S(1)}, bf16[128,1536]{1,0:T(8,128)(2,1)S(1)}, f32[24,1536]{1,0:T(8,128)S(1)}) custom-call(s32[3]{0:T(128)S(1)} %pad_add_fusion.1.info_ref, bf16[128,1664]{1,0:T(8,128)(2,1)S(1)} %copy-done.20, f32[1,1536]{1,0:T(1,128)S(1)} %maximum_convert_fusion.6.gain_ref, ...), custom_call_target="tpu_custom_call" | custom-call | flops 5750000128 | tf_op jit(solution)/shard_map/residual_backward/pallas_call | solution.py:563
  236.1 10.2 %attention_backward.1 = (bf16[128,1536]{1,0:T(8,128)(2,1)S(1)}, bf16[128,1024]{1,0:T(8,128)(2,1)S(1)}, bf16[128,1024]{1,0:T(8,128)(2,1)S(1)}, bf16[128,1024]{1,0...) custom-call(bf16[128,1536]{1,0:T(8,128)(2,1)S(1)} %get-tuple-element, ...), custom_call_target="tpu_custom_call" | custom-call | flops 11500000256 | tf_op jit(solution)/shard_map/attention_backward/pallas_call | solution.py:381
  257.9 6.1 %collective-permute-done.50 = bf16[128,1536]{1,0:T(8,128)(2,1)} collective-permute-done((bf16[128,1536]{1,0:T(8,128)(2,1)}, bf16[128,1536]{1,0:T(8,128)(2,1)}, u32[]{:S(2)}, u32[]{:S(2)}) %collective-permute-start.50) | collective-permute-done | bytes 393248 | tf_op jit(solution)/shard_map/ppermute | solution.py:38
  265.7 9.4 %collective-permute-done.57 = bf16[256,1024]{1,0:T(8,128)(2,1)S(1)} collective-permute-done((bf16[256,1024]{1,0:T(8,128)(2,1)}, bf16[256,1024]{1,0:T(8,128)(2,1)S(1)}, u32[]{:S(2)}, u32[]{:S(2)}) %collective-permute-start.57) | collective-permute-done | bytes 524320 | tf_op jit(solution)/shard_map/ppermute | solution.py:38
  281.2 2.1 convolution_convert_fusion.1
  283.3 9.4 %collective-permute-done.59 = bf16[128,1536]{1,0:T(8,128)(2,1)S(1)} collective-permute-done((bf16[128,1536]{1,0:T(8,128)(2,1)S(1)}, bf16[128,1536]{1,0:T(8,128)(2,1)S(1)}, u32[]{:S(2)}, u32[]{:S(2)}) %collective-permute-start.59) | collective-permute-done | bytes 393248 | tf_op jit(solution)/shard_map/ppermute | solution.py:38
  301.4 8.5 %collective-permute-done.52 = bf16[4,48,1536]{2,1,0:T(8,128)(2,1)S(1)} collective-permute-done((bf16[4,48,1536]{2,1,0:T(8,128)(2,1)S(1)}, bf16[4,48,1536]{2,1,0:T(8,128)(2,1)S(1)}, u32[]{:S(2)}, u32[]{:S(2)}) %collective-permute-start.52) | collective-permute-done | bytes 589856 | tf_op jit(solution)/shard_map/ppermute | solution.py:38
  310.0 7.7 %collective-permute-done.45 = bf16[128,1024]{1,0:T(8,128)(2,1)S(1)} collective-permute-done((bf16[128,1024]{1,0:T(8,128)(2,1)S(1)}, bf16[128,1024]{1,0:T(8,128)(2,1)S(1)}, u32[]{:S(2)}, u32[]{:S(2)}) %collective-permute-start.45) | collective-permute-done | bytes 262176 | tf_op jit(solution)/shard_map/ppermute | solution.py:966
  319.4 3.1 collective-permute-done.61
  322.7 10.2 %collective-permute-done.53 = bf16[128,1024]{1,0:T(8,128)(2,1)S(1)} collective-permute-done((bf16[128,1024]{1,0:T(8,128)(2,1)S(1)}, bf16[128,1024]{1,0:T(8,128)(2,1)S(1)}, u32[]{:S(2)}, u32[]{:S(2)}) %collective-permute-start.53) | collective-permute-done | bytes 262176 | tf_op jit(solution)/shard_map/ppermute | solution.py:966
  333.1 2.4 collective-permute-done.62
  337.6 6.6 %collective-permute-done.64 = bf16[128,1024]{1,0:T(8,128)(2,1)S(1)} collective-permute-done((bf16[128,1024]{1,0:T(8,128)(2,1)S(1)}, bf16[128,1024]{1,0:T(8,128)(2,1)S(1)}, u32[]{:S(2)}, u32[]{:S(2)}) %collective-permute-start.64) | collective-permute-done | bytes 262176 | tf_op jit(solution)/shard_map/ppermute | solution.py:38
  347.2 5.9 %collective-permute-done.65 = bf16[128,768]{1,0:T(8,128)(2,1)S(1)} collective-permute-done((bf16[128,768]{1,0:T(8,128)(2,1)S(1)}, bf16[128,768]{1,0:T(8,128)(2,1)S(1)}, u32[]{:S(2)}, u32[]{:S(2)}) %collective-permute-start.65) | collective-permute-done | bytes 196640 | tf_op jit(solution)/shard_map/ppermute | solution.py:38
  363.4 3.9 collective-permute-done.68
  371.2 2.8 collective-permute-done.72
  374.1 17.2 %collective-permute-start.73 = (f32[19,48]{1,0:T(8,128)S(1)}, f32[19,48]{1,0:T(8,128)S(1)}, u32[]{:S(2)}, u32[]{:S(2)}) collective-permute-start(f32[19,48]{1,0:T(8,128)S(1)} %bitcast.226), channel_id=1, source_target_pairs={{0,8},{4,12},{8,0},{12,4},{16,24},{20,28},{24,16},{28,20},{1,9},{5... | collective-permute-start | bytes 10952 | tf_op jit(solution)/shard_map/ppermute | solution.py:38
  391.3 2.4 collective-permute-start.75
  393.8 2.1 constant_dynamic-slice_fusion.3
  397.6 2.4 fusion.29
  402.3 13.6 %collective-permute-done.76 = bf16[192,2304]{1,0:T(8,128)(2,1)} collective-permute-done((bf16[192,2304]{1,0:T(8,128)(2,1)}, bf16[192,2304]{1,0:T(8,128)(2,1)}, u32[]{:S(2)}, u32[]{:S(2)}) %collective-permute-start.76) | collective-permute-done | bytes 884768 | tf_op jit(solution)/shard_map/ppermute | solution.py:38
  426.6 13.3 %reduce-scatter.8.cloned.1.call-done = bf16[48,4096]{1,0:T(8,128)(2,1)} async-done(((bf16[192,4096]{1,0:T(8,128)(2,1)}), bf16[48,4096]{1,0:T(8,128)(2,1)}) %reduce-scatter.8.cloned.1.call-update) | async-done | bytes 393232 | tf_op jit(solution)/shard_map/reduce_scatter | solution.py:978
  (452 shorter events, 122.6 us)
Async XLA Ops:
  7.2 239.1 %reduce-scatter.4.cloned.1.call-start = ((), (), s32[]{:S(2)}) async-start(), calls=%async_computation.3 | async-start | bytes 4423680 | tf_op jit(solution)/shard_map/reduce_scatter | solution.py:978
  9.5 14.7 %collective-permute-start.2 = (bf16[18,384]{1,0:T(8,128)(2,1)S(1)}, bf16[18,384]{1,0:T(8,128)(2,1)S(1)}, u32[]{:S(2)}, u32[]{:S(2)}) collective-permute-start(bf16[18,384]{1,0:T(8,128)(2,1)S(1)} %pad_maximum_fusion.19), channel_id=1, source_target_pairs={{0,1},{1,0},{2,3},{3,2},{4,5},{5,4},{6,7},{7,6},{8,9},{9,8},{10,11... | collective-permute-start | bytes 41480 | tf_op jit(solution)/shard_map/ppermute | solution.py:38
  10.0 14.2 %collective-permute-start.6 = (bf16[18,384]{1,0:T(8,128)(2,1)S(1)}, bf16[18,384]{1,0:T(8,128)(2,1)S(1)}, u32[]{:S(2)}, u32[]{:S(2)}) collective-permute-start(bf16[18,384]{1,0:T(8,128)(2,1)S(1)} %pad_maximum_fusion.19), channel_id=1, source_target_pairs={{0,2},{1,3},{2,0},{3,1},{4,6},{5,7},{6,4},{7,5},{8,10},{9,11},{10,... | collective-permute-start | bytes 41480 | tf_op jit(solution)/shard_map/ppermute | solution.py:38
  24.2 23.6 %collective-permute-start.3 = (bf16[384,1536]{1,0:T(8,128)(2,1)S(1)}, bf16[384,1536]{1,0:T(8,128)(2,1)S(1)}, u32[]{:S(2)}, u32[]{:S(2)}) collective-permute-start(bf16[384,1536]{1,0:T(8,128)(2,1)S(1)} %copy-done.29), channel_id=1, source_target_pairs={{0,1},{1,0},{2,3},{3,2},{4,5},{5,4},{6,7},{7,6},{8,9},{9,8},{10,11... | collective-permute-start | bytes 3538952 | tf_op jit(solution)/shard_map/ppermute | solution.py:38
  36.6 14.5 %collective-permute-start.17 = (bf16[384,768]{1,0:T(8,128)(2,1)S(1)}, bf16[384,768]{1,0:T(8,128)(2,1)S(1)}, u32[]{:S(2)}, u32[]{:S(2)}) collective-permute-start(bf16[384,768]{1,0:T(8,128)(2,1)S(1)} %copy-done.49), channel_id=1, source_target_pairs={{0,2},{1,3},{2,0},{3,1},{4,6},{5,7},{6,4},{7,5},{8,10},{9,11},{10,... | collective-permute-start | bytes 1769480 | tf_op jit(solution)/shard_map/ppermute | solution.py:38
  37.6 15.8 %collective-permute-start.10 = (bf16[128,1024]{1,0:T(8,128)(2,1)S(1)}, bf16[128,1024]{1,0:T(8,128)(2,1)S(1)}, u32[]{:S(2)}, u32[]{:S(2)}) collective-permute-start(bf16[128,1024]{1,0:T(8,128)(2,1)S(1)} %fusion.39.refs_0_), channel_id=1, source_target_pairs={{0,8},{4,12},{8,16},{12,20},{16,24},{20,28},{1,9},{5,13},{9,17},{1... | collective-permute-start | bytes 786440 | tf_op jit(solution)/shard_map/ppermute | solution.py:952
  41.3 12.8 %collective-permute-start.12 = (bf16[128,1024]{1,0:T(8,128)(2,1)S(1)}, bf16[128,1024]{1,0:T(8,128)(2,1)S(1)}, u32[]{:S(2)}, u32[]{:S(2)}) collective-permute-start(bf16[128,1024]{1,0:T(8,128)(2,1)S(1)} %fusion.39.refs_0_), channel_id=1, source_target_pairs={{0,16},{4,20},{8,24},{12,28},{1,17},{5,21},{9,25},{13,29},{2,18},{... | collective-permute-start | bytes 786440 | tf_op jit(solution)/shard_map/ppermute | solution.py:952
  45.9 12.8 %collective-permute-start.14 = (bf16[128,1024]{1,0:T(8,128)(2,1)S(1)}, bf16[128,1024]{1,0:T(8,128)(2,1)S(1)}, u32[]{:S(2)}, u32[]{:S(2)}) collective-permute-start(bf16[128,1024]{1,0:T(8,128)(2,1)S(1)} %fusion.39.refs_0_), channel_id=1, source_target_pairs={{0,24},{4,28},{1,25},{5,29},{2,26},{6,30},{3,27},{7,31}} | collective-permute-start | bytes 786440 | tf_op jit(solution)/shard_map/ppermute | solution.py:952
  47.7 12.4 %collective-permute-start.9 = (bf16[128,1024]{1,0:T(8,128)(2,1)S(1)}, bf16[128,1024]{1,0:T(8,128)(2,1)S(1)}, u32[]{:S(2)}, u32[]{:S(2)}) collective-permute-start(bf16[128,1024]{1,0:T(8,128)(2,1)S(1)} %fusion.39.refs_0_), channel_id=1, source_target_pairs={{0,4},{4,0},{8,12},{12,8},{16,20},{20,16},{24,28},{28,24},{1,5},{5... | collective-permute-start | bytes 786440 | tf_op jit(solution)/shard_map/ppermute | solution.py:38
  51.1 18.9 %collective-permute-start.18 = (bf16[384,768]{1,0:T(8,128)(2,1)S(1)}, bf16[384,768]{1,0:T(8,128)(2,1)S(1)}, u32[]{:S(2)}, u32[]{:S(2)}) collective-permute-start(bf16[384,768]{1,0:T(8,128)(2,1)S(1)} %collective-permute-done.17), channel_id=1, source_target_pairs={{0,8},{4,12},{8,0},{12,4},{16,24},{20,28},{24,16},{28,20},{1,9},{5... | collective-permute-start | bytes 1769480 | tf_op jit(solution)/shard_map/ppermute | solution.py:38
  54.2 15.9 %collective-permute-start.11 = (bf16[128,1024]{1,0:T(8,128)(2,1)S(1)}, bf16[128,1024]{1,0:T(8,128)(2,1)S(1)}, u32[]{:S(2)}, u32[]{:S(2)}) collective-permute-start(bf16[128,1024]{1,0:T(8,128)(2,1)S(1)} %collective-permute-done.10.refs_2_), channel_id=1, source_target_pairs={{0,4},{4,0},{8,12},{12,8},{16,20},{20,16},{24,28},{28,24},{1,5},{5... | collective-permute-start | bytes 786440 | tf_op jit(solution)/shard_map/ppermute | solution.py:38
  58.7 12.0 %collective-permute-start.13 = (bf16[128,1024]{1,0:T(8,128)(2,1)S(1)}, bf16[128,1024]{1,0:T(8,128)(2,1)S(1)}, u32[]{:S(2)}, u32[]{:S(2)}) collective-permute-start(bf16[128,1024]{1,0:T(8,128)(2,1)S(1)} %collective-permute-done.12.refs_4_), channel_id=1, source_target_pairs={{0,4},{4,0},{8,12},{12,8},{16,20},{20,16},{24,28},{28,24},{1,5},{5... | collective-permute-start | bytes 786440 | tf_op jit(solution)/shard_map/ppermute | solution.py:38
  60.2 11.7 %collective-permute-start.15 = (bf16[128,1024]{1,0:T(8,128)(2,1)S(1)}, bf16[128,1024]{1,0:T(8,128)(2,1)S(1)}, u32[]{:S(2)}, u32[]{:S(2)}) collective-permute-start(bf16[128,1024]{1,0:T(8,128)(2,1)S(1)} %collective-permute-done.14.refs_6_), channel_id=1, source_target_pairs={{0,4},{4,0},{8,12},{12,8},{16,20},{20,16},{24,28},{28,24},{1,5},{5... | collective-permute-start | bytes 786440 | tf_op jit(solution)/shard_map/ppermute | solution.py:38
  62.7 25.1 %collective-permute-start.22 = (bf16[768,768]{1,0:T(8,128)(2,1)S(1)}, bf16[768,768]{1,0:T(8,128)(2,1)S(1)}, u32[]{:S(2)}, u32[]{:S(2)}) collective-permute-start(bf16[768,768]{1,0:T(8,128)(2,1)S(1)} %maximum_maximum_fusion), channel_id=1, source_target_pairs={{0,2},{1,3},{2,0},{3,1},{4,6},{5,7},{6,4},{7,5},{8,10},{9,11},{10,... | collective-permute-start | bytes 3538952 | tf_op jit(solution)/shard_map/ppermute | solution.py:38
  70.0 18.1 %collective-permute-start.16 = (bf16[384,1536]{1,0:T(8,128)(2,1)S(1)}, bf16[384,1536]{1,0:T(8,128)(2,1)S(1)}, u32[]{:S(2)}, u32[]{:S(2)}) collective-permute-start(bf16[384,1536]{1,0:T(8,128)(2,1)S(1)} %copy-done.3), channel_id=1, source_target_pairs={{0,1},{1,0},{2,3},{3,2},{4,5},{5,4},{6,7},{7,6},{8,9},{9,8},{10,11... | collective-permute-start | bytes 3538952 | tf_op jit(solution)/shard_map/ppermute | solution.py:38
  70.0 25.1 %collective-permute-start.24 = (bf16[384,768]{1,0:T(8,128)(2,1)S(1)}, bf16[384,768]{1,0:T(8,128)(2,1)S(1)}, u32[]{:S(2)}, u32[]{:S(2)}) collective-permute-start(bf16[384,768]{1,0:T(8,128)(2,1)S(1)} %pad_maximum_fusion.3), channel_id=1, source_target_pairs={{0,1},{1,0},{2,3},{3,2},{4,5},{5,4},{6,7},{7,6},{8,9},{9,8},{10,11... | collective-permute-start | bytes 1769480 | tf_op jit(solution)/shard_map/ppermute | solution.py:38
  71.9 16.2 %collective-permute-start.19 = (bf16[768,768]{1,0:T(8,128)(2,1)S(1)}, bf16[768,768]{1,0:T(8,128)(2,1)S(1)}, u32[]{:S(2)}, u32[]{:S(2)}) collective-permute-start(bf16[768,768]{1,0:T(8,128)(2,1)S(1)} %constant_dynamic-update-slice_fusion.o2.refs_9_), channel_id=1, source_target_pairs={{0,1},{1,0},{2,3},{3,2},{4,5},{5,4},{6,7},{7,6},{8,9},{9,8},{10,11... | collective-permute-start | bytes 3538952 | tf_op jit(solution)/shard_map/ppermute | solution.py:38
  93.1 13.3 %collective-permute-start.26 = (bf16[128,1664]{1,0:T(8,128)(2,1)S(1)}, bf16[128,1664]{1,0:T(8,128)(2,1)S(1)}, u32[]{:S(2)}, u32[]{:S(2)}) collective-permute-start(bf16[128,1664]{1,0:T(8,128)(2,1)S(1)} %get-tuple-element.92.xa_ref.refs_8_.refs_0_.refs_4_), channel_id=1, source_target_pairs={{0,2},{1,3},{2,0},{3,1},{4,6},{5,7},{6,4},{7,5},{8,10},{9,11},{10,... | collective-permute-start | bytes 1277960 | tf_op jit(solution)/shard_map/ppermute | solution.py:38
  93.7 12.8 %collective-permute-start.27 = (bf16[128,1664]{1,0:T(8,128)(2,1)S(1)}, bf16[128,1664]{1,0:T(8,128)(2,1)}, u32[]{:S(2)}, u32[]{:S(2)}) collective-permute-start(bf16[128,1664]{1,0:T(8,128)(2,1)S(1)} %get-tuple-element.92.xa_ref.refs_8_.refs_0_.refs_4_), channel_id=1, source_target_pairs={{0,4},{4,0},{8,12},{12,8},{16,20},{20,16},{24,28},{28,24},{1,5},{5... | collective-permute-start | bytes 1277960 | tf_op jit(solution)/shard_map/ppermute | solution.py:38
  116.2 12.2 %collective-permute-start.31 = (bf16[128,1664]{1,0:T(8,128)(2,1)S(1)}, bf16[128,1664]{1,0:T(8,128)(2,1)}, u32[]{:S(2)}, u32[]{:S(2)}) collective-permute-start(bf16[128,1664]{1,0:T(8,128)(2,1)S(1)} %collective-permute-done.26.xa_ref.refs_10_.refs_2_), channel_id=1, source_target_pairs={{0,4},{4,0},{8,12},{12,8},{16,20},{20,16},{24,28},{28,24},{1,5},{5... | collective-permute-start | bytes 1277960 | tf_op jit(solution)/shard_map/ppermute | solution.py:38
  119.8 11.5 %collective-permute-start.30 = (bf16[128,1536]{1,0:T(8,128)(2,1)}, bf16[128,1536]{1,0:T(8,128)(2,1)}, u32[]{:S(2)}, u32[]{:S(2)}) collective-permute-start(bf16[128,1536]{1,0:T(8,128)(2,1)} %add_convert_fusion.1), channel_id=1, source_target_pairs={{0,2},{1,3},{2,0},{3,1},{4,6},{5,7},{6,4},{7,5},{8,10},{9,11},{10,... | collective-permute-start | bytes 1179656 | tf_op jit(solution)/shard_map/ppermute | solution.py:38
  121.3 16.3 %collective-permute-start.35 = (bf16[128,1664]{1,0:T(8,128)(2,1)}, bf16[128,1664]{1,0:T(8,128)(2,1)}, u32[]{:S(2)}, u32[]{:S(2)}) collective-permute-start(bf16[128,1664]{1,0:T(8,128)(2,1)} %collective-permute-done.27.x0.e0.refs_4_), channel_id=1, source_target_pairs={{0,1},{1,0},{2,3},{3,2},{4,5},{5,4},{6,7},{7,6},{8,9},{9,8},{10,11... | collective-permute-start | bytes 1277960 | tf_op jit(solution)/shard_map/ppermute | solution.py:38
  135.4 15.9 %collective-permute-start.33 = (bf16[128,1664]{1,0:T(8,128)(2,1)S(1)}, bf16[128,1664]{1,0:T(8,128)(2,1)S(1)}, u32[]{:S(2)}, u32[]{:S(2)}) collective-permute-start(bf16[128,1664]{1,0:T(8,128)(2,1)S(1)} %get-tuple-element.111.refs_0_.refs_4_), channel_id=1, source_target_pairs={{0,2},{1,3},{2,0},{3,1},{4,6},{5,7},{6,4},{7,5},{8,10},{9,11},{10,... | collective-permute-start | bytes 1277960 | tf_op jit(solution)/shard_map/ppermute | solution.py:38
  137.0 14.3 %collective-permute-start.34 = (bf16[128,1664]{1,0:T(8,128)(2,1)S(1)}, bf16[128,1664]{1,0:T(8,128)(2,1)S(1)}, u32[]{:S(2)}, u32[]{:S(2)}) collective-permute-start(bf16[128,1664]{1,0:T(8,128)(2,1)S(1)} %get-tuple-element.111.refs_0_.refs_4_), channel_id=1, source_target_pairs={{0,4},{4,0},{8,12},{12,8},{16,20},{20,16},{24,28},{28,24},{1,5},{5... | collective-permute-start | bytes 1277960 | tf_op jit(solution)/shard_map/ppermute | solution.py:38
  173.2 220.6 %reduce-scatter.6.cloned.1.call-start = ((), (), s32[]{:S(2)}) async-start(), calls=%async_computation.4 | async-start | bytes 8847360 | tf_op jit(solution)/shard_map/reduce_scatter | solution.py:978
  201.9 29.1 %collective-permute-start.43 = (bf16[128,1664]{1,0:T(8,128)(2,1)}, bf16[128,1664]{1,0:T(8,128)(2,1)}, u32[]{:S(2)}, u32[]{:S(2)}) collective-permute-start(bf16[128,1664]{1,0:T(8,128)(2,1)} %get-tuple-element.128), channel_id=1, source_target_pairs={{0,1},{1,0},{2,3},{3,2},{4,5},{5,4},{6,7},{7,6},{8,9},{9,8},{10,11... | collective-permute-start | bytes 1277960 | tf_op jit(solution)/shard_map/ppermute | solution.py:38
  203.7 11.9 %collective-permute-start.42 = (bf16[128,1664]{1,0:T(8,128)(2,1)S(1)}, bf16[128,1664]{1,0:T(8,128)(2,1)S(1)}, u32[]{:S(2)}, u32[]{:S(2)}) collective-permute-start(bf16[128,1664]{1,0:T(8,128)(2,1)S(1)} %add_convert_fusion), channel_id=1, source_target_pairs={{0,2},{1,3},{2,0},{3,1},{4,6},{5,7},{6,4},{7,5},{8,10},{9,11},{10,... | collective-permute-start | bytes 1277960 | tf_op jit(solution)/shard_map/ppermute | solution.py:38
  246.4 193.5 %reduce-scatter.8.cloned.1.call-start = ((), (), s32[]{:S(2)}) async-start(), calls=%async_computation.5 | async-start | bytes 1966080 | tf_op jit(solution)/shard_map/reduce_scatter | solution.py:978
  250.4 15.1 %collective-permute-start.44 = (bf16[256,1024]{1,0:T(8,128)(2,1)}, bf16[256,1024]{1,0:T(8,128)(2,1)S(1)}, u32[]{:S(2)}, u32[]{:S(2)}) collective-permute-start(bf16[256,1024]{1,0:T(8,128)(2,1)} %pad_maximum_fusion.6), channel_id=1, source_target_pairs={{0,4},{4,0},{8,12},{12,8},{16,20},{20,16},{24,28},{28,24},{1,5},{5... | collective-permute-start | bytes 1572872 | tf_op jit(solution)/shard_map/ppermute | solution.py:38
  253.9 26.7 %collective-permute-start.49 = (bf16[128,1536]{1,0:T(8,128)(2,1)}, bf16[128,1536]{1,0:T(8,128)(2,1)}, u32[]{:S(2)}, u32[]{:S(2)}) collective-permute-start(bf16[128,1536]{1,0:T(8,128)(2,1)} %get-tuple-element.140.attn_ref), channel_id=1, source_target_pairs={{0,1},{1,0},{2,3},{3,2},{4,5},{5,4},{6,7},{7,6},{8,9},{9,8},{10,11... | collective-permute-start | bytes 1179656 | tf_op jit(solution)/shard_map/ppermute | solution.py:38
  255.0 20.1 %collective-permute-start.57 = (bf16[256,1024]{1,0:T(8,128)(2,1)}, bf16[256,1024]{1,0:T(8,128)(2,1)S(1)}, u32[]{:S(2)}, u32[]{:S(2)}) collective-permute-start(bf16[256,1024]{1,0:T(8,128)(2,1)} %pad_maximum_fusion.7), channel_id=1, source_target_pairs={{0,4},{4,0},{8,12},{12,8},{16,20},{20,16},{24,28},{28,24},{1,5},{5... | collective-permute-start | bytes 1572872 | tf_op jit(solution)/shard_map/ppermute | solution.py:38
  256.7 18.5 %collective-permute-start.46 = (bf16[128,384]{0,1:T(8,128)(2,1)}, bf16[128,384]{0,1:T(8,128)(2,1)}, u32[]{:S(2)}, u32[]{:S(2)}) collective-permute-start(bf16[128,384]{0,1:T(8,128)(2,1)} %get-tuple-element.211), channel_id=1, source_target_pairs={{0,1},{1,0},{2,3},{3,2},{4,5},{5,4},{6,7},{7,6},{8,9},{9,8},{10,11... | collective-permute-start | bytes 294920 | tf_op jit(solution)/shard_map/ppermute | solution.py:38
  264.1 11.9 %collective-permute-start.47 = (bf16[128,384]{0,1:T(8,128)(2,1)}, bf16[128,384]{0,1:T(8,128)(2,1)S(1)}, u32[]{:S(2)}, u32[]{:S(2)}) collective-permute-start(bf16[128,384]{0,1:T(8,128)(2,1)} %get-tuple-element.210), channel_id=1, source_target_pairs={{0,2},{1,3},{2,0},{3,1},{4,6},{5,7},{6,4},{7,5},{8,10},{9,11},{10,... | collective-permute-start | bytes 294920 | tf_op jit(solution)/shard_map/ppermute | solution.py:38
  265.5 15.3 %collective-permute-start.51 = (bf16[128,1536]{1,0:T(8,128)(2,1)}, bf16[128,1536]{1,0:T(8,128)(2,1)S(1)}, u32[]{:S(2)}, u32[]{:S(2)}) collective-permute-start(bf16[128,1536]{1,0:T(8,128)(2,1)} %collective-permute-done.50), channel_id=1, source_target_pairs={{0,1},{1,0},{2,3},{3,2},{4,5},{5,4},{6,7},{7,6},{8,9},{9,8},{10,11... | collective-permute-start | bytes 1179656 | tf_op jit(solution)/shard_map/ppermute | solution.py:38
  275.2 18.5 %collective-permute-start.54 = (bf16[128,384]{0,1:T(8,128)(2,1)S(1)}, bf16[128,384]{0,1:T(8,128)(2,1)S(1)}, u32[]{:S(2)}, u32[]{:S(2)}) collective-permute-start(bf16[128,384]{0,1:T(8,128)(2,1)S(1)} %copy-done.66), channel_id=1, source_target_pairs={{0,1},{1,0},{2,3},{3,2},{4,5},{5,4},{6,7},{7,6},{8,9},{9,8},{10,11... | collective-permute-start | bytes 294920 | tf_op jit(solution)/shard_map/ppermute | solution.py:38
  275.9 19.1 %collective-permute-start.55 = (bf16[128,384]{0,1:T(8,128)(2,1)S(1)}, bf16[128,384]{0,1:T(8,128)(2,1)S(1)}, u32[]{:S(2)}, u32[]{:S(2)}) collective-permute-start(bf16[128,384]{0,1:T(8,128)(2,1)S(1)} %copy-done.65), channel_id=1, source_target_pairs={{0,2},{1,3},{2,0},{3,1},{4,6},{5,7},{6,4},{7,5},{8,10},{9,11},{10,... | collective-permute-start | bytes 294920 | tf_op jit(solution)/shard_map/ppermute | solution.py:38
  279.3 17.0 %collective-permute-start.56 = (bf16[128,384]{0,1:T(8,128)(2,1)S(1)}, bf16[128,384]{0,1:T(8,128)(2,1)S(1)}, u32[]{:S(2)}, u32[]{:S(2)}) collective-permute-start(bf16[128,384]{0,1:T(8,128)(2,1)S(1)} %copy-done.64), channel_id=1, source_target_pairs={{0,3},{1,2},{2,1},{3,0},{4,7},{5,6},{6,5},{7,4},{8,11},{9,10},{10,... | collective-permute-start | bytes 294920 | tf_op jit(solution)/shard_map/ppermute | solution.py:38
  280.6 12.2 %collective-permute-start.59 = (bf16[128,1536]{1,0:T(8,128)(2,1)S(1)}, bf16[128,1536]{1,0:T(8,128)(2,1)S(1)}, u32[]{:S(2)}, u32[]{:S(2)}) collective-permute-start(bf16[128,1536]{1,0:T(8,128)(2,1)S(1)} %get-tuple-element.145), channel_id=1, source_target_pairs={{0,2},{1,3},{2,0},{3,1},{4,6},{5,7},{6,4},{7,5},{8,10},{9,11},{10,... | collective-permute-start | bytes 1179656 | tf_op jit(solution)/shard_map/ppermute | solution.py:38
  280.8 16.9 %collective-permute-start.58 = (bf16[128,1536]{1,0:T(8,128)(2,1)S(1)}, bf16[128,1536]{1,0:T(8,128)(2,1)S(1)}, u32[]{:S(2)}, u32[]{:S(2)}) collective-permute-start(bf16[128,1536]{1,0:T(8,128)(2,1)S(1)} %get-tuple-element.145), channel_id=1, source_target_pairs={{0,1},{1,0},{2,3},{3,2},{4,5},{5,4},{6,7},{7,6},{8,9},{9,8},{10,11... | collective-permute-start | bytes 1179656 | tf_op jit(solution)/shard_map/ppermute | solution.py:38
  293.7 16.2 %collective-permute-start.52 = (bf16[4,48,1536]{2,1,0:T(8,128)(2,1)S(1)}, bf16[4,48,1536]{2,1,0:T(8,128)(2,1)S(1)}, u32[]{:S(2)}, u32[]{:S(2)}) collective-permute-start(bf16[4,48,1536]{2,1,0:T(8,128)(2,1)S(1)} %dynamic-slice_bitcast_fusion.1), channel_id=1, source_target_pairs={{0,4},{4,0},{8,12},{12,8},{16,20},{20,16},{24,28},{28,24},{1,5},{5... | collective-permute-start | bytes 1769480 | tf_op jit(solution)/shard_map/ppermute | solution.py:38
  295.0 22.8 %collective-permute-start.45 = (bf16[128,1024]{1,0:T(8,128)(2,1)S(1)}, bf16[128,1024]{1,0:T(8,128)(2,1)S(1)}, u32[]{:S(2)}, u32[]{:S(2)}) collective-permute-start(bf16[128,1024]{1,0:T(8,128)(2,1)S(1)} %get-tuple-element.191), channel_id=1, source_target_pairs={{24,0},{28,4},{25,1},{29,5},{26,2},{30,6},{27,3},{31,7}} | collective-permute-start | bytes 786440 | tf_op jit(solution)/shard_map/ppermute | solution.py:966
  296.4 36.6 %collective-permute-start.53 = (bf16[128,1024]{1,0:T(8,128)(2,1)S(1)}, bf16[128,1024]{1,0:T(8,128)(2,1)S(1)}, u32[]{:S(2)}, u32[]{:S(2)}) collective-permute-start(bf16[128,1024]{1,0:T(8,128)(2,1)S(1)} %get-tuple-element.192), channel_id=1, source_target_pairs={{16,0},{20,4},{24,8},{28,12},{17,1},{21,5},{25,9},{29,13},{18,2},{... | collective-permute-start | bytes 786440 | tf_op jit(solution)/shard_map/ppermute | solution.py:966
  297.7 37.9 %collective-permute-start.62 = (bf16[128,1024]{1,0:T(8,128)(2,1)S(1)}, bf16[128,1024]{1,0:T(8,128)(2,1)S(1)}, u32[]{:S(2)}, u32[]{:S(2)}) collective-permute-start(bf16[128,1024]{1,0:T(8,128)(2,1)S(1)} %add_convert_fusion.3), channel_id=1, source_target_pairs={{8,0},{12,4},{16,8},{20,12},{24,16},{28,20},{9,1},{13,5},{17,9},{2... | collective-permute-start | bytes 786440 | tf_op jit(solution)/shard_map/ppermute | solution.py:966
  300.0 22.5 %collective-permute-start.61 = (bf16[4,48,1536]{2,1,0:T(8,128)(2,1)S(1)}, bf16[4,48,1536]{2,1,0:T(8,128)(2,1)S(1)}, u32[]{:S(2)}, u32[]{:S(2)}) collective-permute-start(bf16[4,48,1536]{2,1,0:T(8,128)(2,1)S(1)} %dynamic-slice_bitcast_fusion), channel_id=1, source_target_pairs={{0,4},{4,0},{8,12},{12,8},{16,20},{20,16},{24,28},{28,24},{1,5},{5... | collective-permute-start | bytes 1769480 | tf_op jit(solution)/shard_map/ppermute | solution.py:38
  317.8 15.1 %collective-permute-start.63 = (bf16[192,1152]{1,0:T(8,128)(2,1)S(1)}, bf16[192,1152]{1,0:T(8,128)(2,1)S(1)}, u32[]{:S(2)}, u32[]{:S(2)}) collective-permute-start(bf16[192,1152]{1,0:T(8,128)(2,1)S(1)} %constant_dynamic-slice_fusion.14), channel_id=1, source_target_pairs={{0,4},{4,0},{8,12},{12,8},{16,20},{20,16},{24,28},{28,24},{1,5},{5... | collective-permute-start | bytes 1327112 | tf_op jit(solution)/shard_map/ppermute | solution.py:38
  335.9 19.6 %collective-permute-start.66 = (bf16[128,1024]{1,0:T(8,128)(2,1)S(1)}, bf16[128,1024]{1,0:T(8,128)(2,1)}, u32[]{:S(2)}, u32[]{:S(2)}) collective-permute-start(bf16[128,1024]{1,0:T(8,128)(2,1)S(1)} %add_convert_fusion.2), channel_id=1, source_target_pairs={{0,1},{1,0},{2,3},{3,2},{4,5},{5,4},{6,7},{7,6},{8,9},{9,8},{10,11... | collective-permute-start | bytes 786440 | tf_op jit(solution)/shard_map/ppermute | solution.py:38
  374.1 25.9 %collective-permute-start.73 = (f32[19,48]{1,0:T(8,128)S(1)}, f32[19,48]{1,0:T(8,128)S(1)}, u32[]{:S(2)}, u32[]{:S(2)}) collective-permute-start(f32[19,48]{1,0:T(8,128)S(1)} %bitcast.226), channel_id=1, source_target_pairs={{0,8},{4,12},{8,0},{12,4},{16,24},{20,28},{24,16},{28,20},{1,9},{5... | collective-permute-start | bytes 10952 | tf_op jit(solution)/shard_map/ppermute | solution.py:38
  395.9 20.0 %collective-permute-start.76 = (bf16[192,2304]{1,0:T(8,128)(2,1)}, bf16[192,2304]{1,0:T(8,128)(2,1)}, u32[]{:S(2)}, u32[]{:S(2)}) collective-permute-start(bf16[192,2304]{1,0:T(8,128)(2,1)} %constant_dynamic-slice_fusion.3), channel_id=1, source_target_pairs={{0,4},{4,0},{8,12},{12,8},{16,20},{20,16},{24,28},{28,24},{1,5},{5... | collective-permute-start | bytes 2654216 | tf_op jit(solution)/shard_map/ppermute | solution.py:38
  (123 other events, 1211.4 us)
Sparse Core Ops, SparseCore 0:
  173.3 71.2 reduce-scatter.3
  246.9 145.0 reduce-scatter.5
  401.9 38.0 reduce-scatter.7
where the time goes:
time: 455 us; the launch traced here: 451 us
  waiting for transfers between devices  169 us (37%)
  Pallas kernels  105 us (23%)
  starting transfers between devices  78.5 us (17%)
  local copies, waits for them, and re-layouts  42.6 us (9%)
  other arithmetic  25.7 us (6%)
  between operations  18.5 us (4%)
  matrix products  12.7 us (3%)
    ppermute x74, waiting for transfers between devices, swap(): return lax.ppermute(value, axis, [(i, i ^ bit) for i in range(size)])  132 us
    ppermute x74, starting transfers between devices, swap(): return lax.ppermute(value, axis, [(i, i ^ bit) for i in range(size)])  64.5 us
    pallas_call x2, Pallas kernels, weight_grad_call(): pl.pallas_call(weight_grad_kernel, out_shape=hbm((features, held // rows...  23.3 us
    ppermute x3, waiting for transfers between devices, sum_key_blocks(): lax.ppermute(level.astype(bf16), 'ctx', [(i + 2 * s, i) for i in range(n...  20.4 us
    unnamed x194, local copies, waits for them, and re-layouts  20.4 us
    pallas_call x1, Pallas kernels, experts_back_call(): pl.pallas_call(experts_back_kernel, out_shape=(hbm(ext, f32), jax.ShapeDt...  20.2 us
    pallas_call x2, Pallas kernels, experts_call(): pl.pallas_call(experts_kernel, out_shape=(hbm((rows, features), f32), jax...  15.9 us
    reduce_scatter x3, waiting for transfers between devices, sum_pairs(): lax.psum_scatter(value, 'ctx', scatter_dimension=0, tiled=True, axis_inde...  13.3 us
  transfers between devices with their start and end apart: 83, of which 34 were waited for; matrix products, arithmetic and copies ran while one was open for 13% of the time, Pallas kernels for 20%

commit v1 on v0

--- a/solution.py
+++ b/solution.py
@@ -675,9 +675,11 @@
 
 
 def experts_back_kernel(info_ref, *refs):
-    (gate_ref, up_ref, down_ref, shared_ref), refs = refs[:4], refs[4:]
+    shared_ref, weights_in, refs = refs[0], refs[1:4], refs[4:]
     g_in, e_in, (gpa_in, gpb_in, upa_in, upb_in), refs = refs[:4], refs[4:8], refs[8:12], refs[12:]
     (dxa_hbm, dxb_ref, dxc_ref, dxd_ref, dg_out, du_out), refs = refs[:6], refs[6:]
+    held, refs = refs[:3], refs[3:]
+    gate_ref, up_ref, down_ref = held
     gp_ref, upre_ref, dg_ref, du_ref, g_ref, extra_ref, dxa_ref, acc_ref, sems = refs
     rows = g_in[0].shape[0]
     features = g_ref.shape[1]
@@ -685,6 +687,10 @@
     x = info_ref[1]
     first, last = pl.ds(0, 2 * rows), pl.ds(2 * rows, 2 * rows)
     loads = load_rows(g_in, g_ref, None, sems, 0)
+    weight_loads = [
+        [start_copy(weights_in[i].at[e], held[i].at[e], sems, 19 + 3 * e + i) for i in (2, 0, 1)]
+        for e in range(1)
+    ]
     late = [
         start_copy(source, target, sems, 8 + i)
         for i, (source, target) in enumerate(
@@ -700,6 +706,10 @@
         at = pl.ds(i * rows, rows)
         source = e_in[i].at[:, pl.ds(features, EXTRA)]
         late.append(start_copy(source, extra_ref.at[at], sems, 12 + i))
+    weight_loads += [
+        [start_copy(weights_in[i].at[e], held[i].at[e], sems, 19 + 3 * e + i) for i in (2, 0, 1)]
+        for e in range(1, here)
+    ]
     wait_all(loads)
     s_gate, s_up, s_down = shared_parts_of(shared_ref)
     spans = [slice(i * 2 * rows, (i + 1) * 2 * rows) for i in range(2)]
@@ -727,6 +737,7 @@
         expert = info_ref[0] * here + e
         half, at = e // 2, (e % 2) * width
         cols = slice(at, at + width)
+        wait_all(weight_loads[e])
         for i, span in enumerate(spans):
             d_gate, d_gate_pre, d_up_pre = hidden_back(
                 mm(g_ref[span], down_ref[e]),
@@ -766,20 +777,21 @@
             jax.ShapeDtypeStruct(ext, bf16),
         )
         + (hbm((2 * held, wide), bf16),) * 2,
-        in_specs=[in_smem] + [in_vmem] * 4 + [anywhere] * 12,
+        in_specs=[in_smem, in_vmem] + [anywhere] * 15,
         out_specs=(anywhere,) + (in_vmem,) * 3 + (anywhere,) * 2,
-        scratch_shapes=[pltpu.VMEM((2, 2 * held, wide), bf16)] * 4
+        scratch_shapes=[pltpu.VMEM(weights[0].shape, bf16)] * 3
+        + [pltpu.VMEM((2, 2 * held, wide), bf16)] * 4
         + [
             pltpu.VMEM((4 * rows, features), bf16),
             pltpu.VMEM((4 * rows, EXTRA), bf16),
             pltpu.VMEM(ext, f32),
             pltpu.VMEM((4 * rows, features), f32),
-            pltpu.SemaphoreType.DMA((19,)),
+            pltpu.SemaphoreType.DMA((19 + 3 * weights[0].shape[0],)),
         ],
-        compiler_params=limits(24),
+        compiler_params=limits(46),
         cost_estimate=cost(24),
         name="experts_backward",
-    )(info, *weights, *[in_hbm(value) for value in (*grads, *exts, *kept)])
+    )(info, weights[3], *[in_hbm(value) for value in (*weights[:3], *grads, *exts, *kept)])
 
 
 def pair_shared(info_ref, shared_ref, which):
@@ -788,16 +800,25 @@
     return shared_ref[:, pl.ds(pl.multiple_of(first, 128), width // 2)]
 
 
-def pair_kernel(info_ref, gate_ref, up_ref, shared_ref, x0, x1, x2, x3,
-                gp_out, upre_out, hid_out, gp_ref, upre_ref, hid_ref, x_ref, extra_ref, sems):
-    here, _, width = gate_ref.shape
+def pair_kernel(info_ref, shared_ref, gate_in, up_in, x0, x1, x2, x3, gp_out, upre_out, hid_out,
+                gate_ref, up_ref, gp_ref, upre_ref, hid_ref, x_ref, extra_ref, sems):
+    here, _, width = gate_in.shape
     count = here // 2
-    wait_all(load_rows((x0, x1, x2, x3), x_ref, extra_ref, sems, 3))
+    loads = load_rows((x0, x1, x2, x3), x_ref, extra_ref, sems, 3)
+    weight_loads = [
+        [
+            start_copy(source.at[info_ref[1] * count + j], target.at[j], sems, 11 + 2 * j + i)
+            for i, (source, target) in enumerate([(gate_in, gate_ref), (up_in, up_ref)])
+        ]
+        for j in range(count)
+    ]
+    wait_all(loads)
     extra = extra_ref[...].astype(f32)
     lane = lanes_of(extra.shape[0])
     for j in range(count + 1):
         if j < count:
-            gate_w, up_w = gate_ref[info_ref[1] * count + j], up_ref[info_ref[1] * count + j]
+            wait_all(weight_loads[j])
+            gate_w, up_w = gate_ref[j], up_ref[j]
         else:
             gate_w, up_w = (pair_shared(info_ref, shared_ref, i) for i in range(2))
         gate_pre, up_pre = mm(x_ref[...], gate_w), mm(x_ref[...], up_w)
@@ -826,26 +847,31 @@
     return pl.pallas_call(
         pair_kernel,
         out_shape=(hbm(wide, bf16),) * 3,
-        in_specs=[in_smem] + [in_vmem] * 3 + [anywhere] * 4,
+        in_specs=[in_smem, in_vmem] + [anywhere] * 6,
         out_specs=(anywhere,) * 3,
-        scratch_shapes=[pltpu.VMEM(wide, bf16)] * 3
+        scratch_shapes=[pltpu.VMEM((e_gate.shape[0] // 2,) + e_gate.shape[1:], bf16)] * 2
+        + [pltpu.VMEM(wide, bf16)] * 3
         + [
             pltpu.VMEM((rows, features), bf16),
             pltpu.VMEM((rows, EXTRA), bf16),
-            pltpu.SemaphoreType.DMA((11,)),
+            pltpu.SemaphoreType.DMA((11 + e_gate.shape[0],)),
         ],
-        compiler_params=limits(16),
+        compiler_params=limits(24),
         cost_estimate=cost(8),
         name="pair_forward",
-    )(info, e_gate, e_up, shared, *[in_hbm(value) for value in exts])
-
-
-def pair_back_kernel(info_ref, down_ref, shared_ref, g0, g1, g2, g3, e0, e1, e2, e3, gp_in, upre_in,
-                     dg_out, du_out, gp_ref, upre_ref, dg_ref, du_ref, g_ref, extra_ref, sems):
+    )(info, shared, *[in_hbm(value) for value in (e_gate, e_up, *exts)])
+
+
+def pair_back_kernel(info_ref, shared_ref, down_in, g0, g1, g2, g3, e0, e1, e2, e3, gp_in, upre_in,
+                     dg_out, du_out, down_ref, gp_ref, upre_ref, dg_ref, du_ref, g_ref, extra_ref, sems):
     rows, features = g0.shape[0], g_ref.shape[1]
-    here, _, width = down_ref.shape
+    here, _, width = down_in.shape
     count = here // 2
     loads = load_rows((g0, g1, g2, g3), g_ref, None, sems, 4)
+    weight_loads = [
+        start_copy(down_in.at[info_ref[1] * count + j], down_ref.at[j], sems, 16 + j)
+        for j in range(count)
+    ]
     loads += [start_copy(gp_in, gp_ref, sems, 0), start_copy(upre_in, upre_ref, sems, 1)]
     for i, source in enumerate((e0, e1, e2, e3)):
         lanes = source.at[:, pl.ds(features, EXTRA)]
@@ -856,7 +882,8 @@
     for j in range(count + 1):
         gate = None
         if j < count:
-            weight = down_ref[info_ref[1] * count + j]
+            weight_loads[j].wait()
+            weight = down_ref[j]
             gate = gate_column(extra, lane, info_ref[0] * here + info_ref[1] * count + j)
         else:
             weight = pair_shared(info_ref, shared_ref, 2)
@@ -875,44 +902,58 @@
     return pl.pallas_call(
         pair_back_kernel,
         out_shape=(hbm(wide, bf16),) * 2,
-        in_specs=[in_smem] + [in_vmem] * 2 + [anywhere] * 10,
+        in_specs=[in_smem, in_vmem] + [anywhere] * 11,
         out_specs=(anywhere,) * 2,
-        scratch_shapes=[pltpu.VMEM(wide, bf16)] * 4
+        scratch_shapes=[pltpu.VMEM((weights[2].shape[0] // 2,) + weights[2].shape[1:], bf16)]
+        + [pltpu.VMEM(wide, bf16)] * 4
         + [
             pltpu.VMEM((rows, features), bf16),
             pltpu.VMEM((rows, EXTRA), bf16),
-            pltpu.SemaphoreType.DMA((16,)),
+            pltpu.SemaphoreType.DMA((16 + weights[2].shape[0] // 2,)),
         ],
-        compiler_params=limits(16),
+        compiler_params=limits(20),
         cost_estimate=cost(7),
         name="pair_backward",
-    )(info, weights[2], weights[3], *[in_hbm(value) for value in (*grads, *exts, gate_pre, up_pre)])
+    )(
+        info,
+        weights[3],
+        *[in_hbm(value) for value in (weights[2], *grads, *exts, gate_pre, up_pre)],
+    )
 
 
 def weight_grad_kernel(*refs):
     lefts, rights, (out_ref, left_ref, right_ref, tiles_ref, sems) = refs[:8], refs[8:-5], refs[-5:]
-    features = left_ref.shape[1]
-    loads, at = load_rows(lefts, left_ref, None, sems, 3), 0
+    count, rows, tile = left_ref.shape
+    slots, _, wide = tiles_ref.shape
+    loads, at = [], 0
     for i, ref in enumerate(rights):
         target = right_ref.at[pl.ds(at, ref.shape[0])]
-        loads.append(start_copy(ref, target, sems, 19 + i))
+        loads.append(start_copy(ref, target, sems, slots + i))
         at += ref.shape[0]
+    columns = []
+    for t in range(count):
+        at, first = 0, slots + len(rights) + t * len(lefts)
+        columns.append([])
+        for i, ref in enumerate(lefts):
+            source = ref.at[:, pl.ds(t * tile, tile)]
+            target = left_ref.at[t, pl.ds(at, ref.shape[0])]
+            columns[t].append(start_copy(source, target, sems, first + i))
+            at += ref.shape[0]
     wait_all(loads)
-    rows = left_ref.shape[0]
-    tile, wide = tiles_ref.shape[1:]
     sent = []
     for group in range(right_ref.shape[0] // rows):
         right = slice(group * rows, (group + 1) * rows)
-        for t in range(features // tile):
-            cols = slice(t * tile, (t + 1) * tile)
-            index = group * (features // tile) + t
-            slot = index % tiles_ref.shape[0]
-            if len(sent) >= tiles_ref.shape[0]:
-                sent[index - tiles_ref.shape[0]].wait()
-            tiles_ref[slot] = mm_tn(left_ref[:, cols], right_ref[right]).astype(bf16)
+        for t in range(count):
+            if group == 0:
+                wait_all(columns[t])
+            index = group * count + t
+            slot = index % slots
+            if index >= slots:
+                sent[index - slots].wait()
+            tiles_ref[slot] = mm_tn(left_ref[t], right_ref[right]).astype(bf16)
             target = out_ref.at[pl.ds(t * tile, tile), pl.ds(group * wide, wide)]
             sent.append(start_copy(tiles_ref.at[slot], target, sems, slot))
-    wait_all(sent[-tiles_ref.shape[0] :])
+    wait_all(sent[-slots:])
 
 
 def weight_grad_call(lefts, rights):
@@ -926,10 +967,10 @@
         in_specs=[anywhere] * len(operands),
         out_specs=anywhere,
         scratch_shapes=[
-            pltpu.VMEM((rows, features), bf16),
+            pltpu.VMEM((features // 256, rows, 256), bf16),
             pltpu.VMEM((held, wide), bf16),
             pltpu.VMEM((3, 256, wide), bf16),
-            pltpu.SemaphoreType.DMA((19 + len(rights),)),
+            pltpu.SemaphoreType.DMA((3 + len(rights) + features // 256 * len(lefts),)),
         ],
         compiler_params=limits(16),
         cost_estimate=cost(8 * held // rows),

time: 455 us -> 446 us (0.980)
  local copies, waits for them, and re-layouts: 42.6 us -> 28.6 us
    unnamed x194 -> x184, local copies, waits for them, and re-layouts: 20.4 us -> 6.47 us
    reduce_scatter x3, waiting for transfers between devices: 13.3 us -> 19.2 us  [sum_pairs(): lax.psum_scatter(value, 'ctx', scatter_dimension=0, tiled=True, axis_inde...]
    ppermute x3, waiting for transfers between devices: 20.4 us -> 14.9 us  [sum_key_blocks(): lax.ppermute(level.astype(bf16), 'ctx', [(i + 2 * s, i) for i in range(n...]
  transfers between devices with their start and end apart: 83 -> 83, of which waited for: 34 -> 34; matrix products, arithmetic and copies ran while one was open for 13% -> 13% of each run, Pallas kernels for 20% -> 21%
where the time goes in v1:
time: 446 us; the launch traced here: 442 us
  waiting for transfers between devices  172 us (39%)
  Pallas kernels  108 us (24%)
  starting transfers between devices  76.8 us (17%)
  local copies, waits for them, and re-layouts  28.6 us (6%)
  other arithmetic  25.7 us (6%)
  between operations  18.4 us (4%)
  matrix products  12.7 us (3%)
    ppermute x74, waiting for transfers between devices, swap(): return lax.ppermute(value, axis, [(i, i ^ bit) for i in range(size)])  135 us
    ppermute x74, starting transfers between devices, swap(): return lax.ppermute(value, axis, [(i, i ^ bit) for i in range(size)])  62.8 us
    pallas_call x2, Pallas kernels, weight_grad_call(): pl.pallas_call(weight_grad_kernel, out_shape=hbm((features, held // rows...  22.9 us
    pallas_call x1, Pallas kernels, experts_back_call(): pl.pallas_call(experts_back_kernel, out_shape=(hbm(ext, f32), jax.ShapeDt...  21.2 us
    reduce_scatter x3, waiting for transfers between devices, sum_pairs(): lax.psum_scatter(value, 'ctx', scatter_dimension=0, tiled=True, axis_inde...  19.2 us
    pallas_call x2, Pallas kernels, experts_call(): pl.pallas_call(experts_kernel, out_shape=(hbm((rows, features), f32), jax...  15.9 us
    ppermute x3, waiting for transfers between devices, sum_key_blocks(): lax.ppermute(level.astype(bf16), 'ctx', [(i + 2 * s, i) for i in range(n...  14.9 us
    dot_general x15, matrix products, dot(): lax.dot_general(a, b, ((dims[0], dims[1]), ((), ())), preferred_element_t...  12.7 us
  transfers between devices with their start and end apart: 83, of which 34 were waited for; matrix products, arithmetic and copies ran while one was open for 13% of the time, Pallas kernels for 21%

profile of v1, /device:TPU:0, one launch (start us, length us, event | category | flops | bytes accessed | tf_op | source)
XLA Modules:
  0.0 442.4 jit_solution(15071251863446481482)
XLA Ops:
  10.0 2.6 collective-permute-start.6
  15.5 2.0 collective-permute-start.1
  28.7 7.9 %collective-permute-done.7 = bf16[128,1024]{1,0:T(8,128)(2,1)S(1)} collective-permute-done((bf16[128,1024]{1,0:T(8,128)(2,1)S(1)}, bf16[128,1024]{1,0:T(8,128)(2,1)S(1)}, u32[]{:S(2)}, u32[]{:S(2)}) %collective-permute-start.7) | collective-permute-done | bytes 262176 | tf_op jit(solution)/shard_map/ppermute | solution.py:38
  37.6 3.7 collective-permute-start.10
  41.3 4.5 %collective-permute-start.12 = (bf16[128,1024]{1,0:T(8,128)(2,1)S(1)}, bf16[128,1024]{1,0:T(8,128)(2,1)S(1)}, u32[]{:S(2)}, u32[]{:S(2)}) collective-permute-start(bf16[128,1024]{1,0:T(8,128)(2,1)S(1)} %fusion.39.refs_0_), channel_id=1, source_target_pairs={{0,16},{4,20},{8,24},{12,28},{1,17},{5,21},{9,25},{13,29},{2,18},{... | collective-permute-start | bytes 786440 | tf_op jit(solution)/shard_map/ppermute | solution.py:993
  55.7 2.9 collective-permute-done.14.refs_6_
  60.7 2.0 collective-permute-done.8
  63.3 6.7 %collective-permute-done.18 = bf16[384,768]{1,0:T(8,128)(2,1)S(1)} collective-permute-done((bf16[384,768]{1,0:T(8,128)(2,1)S(1)}, bf16[384,768]{1,0:T(8,128)(2,1)S(1)}, u32[]{:S(2)}, u32[]{:S(2)}) %collective-permute-start.18) | collective-permute-done | bytes 589856 | tf_op jit(solution)/shard_map/ppermute | solution.py:38
  72.0 5.8 %attention_forward.1 = (bf16[128,1536]{1,0:T(8,128)(2,1)}, f32[128,1536]{1,0:T(8,128)}, bf16[4,8,384,128]{3,2,1,0:T(8,128)(2,1)}) custom-call(s32[10]{0:T(128)S(1)} %stack.146.info_ref, bf16[128,1536]{1,0:T(8,128)(2,1)S(1)} %fusion.32.q_ref.q_in, bf16[128,1024]{1,0:T(8,128)(2,1)S(1)} %fusion.39.refs_0_, ...), custom_call_target="tpu_custom_call" | custom-call | flops 5750000128 | tf_op jit(solution)/shard_map/attention_forward/pallas_call | solution.py:313
  77.9 9.9 %collective-permute-done.22 = bf16[768,768]{1,0:T(8,128)(2,1)S(1)} collective-permute-done((bf16[768,768]{1,0:T(8,128)(2,1)S(1)}, bf16[768,768]{1,0:T(8,128)(2,1)S(1)}, u32[]{:S(2)}, u32[]{:S(2)}) %collective-permute-start.22) | collective-permute-done | bytes 1179680 | tf_op jit(solution)/shard_map/ppermute | solution.py:38
  88.2 4.9 %branch_and_router.1 = (f32[128,1536]{1,0:T(8,128)}, bf16[128,1664]{1,0:T(8,128)(2,1)S(1)}, f32[128,128]{1,0:T(8,128)S(1)}) custom-call(s32[3]{0:T(128)S(1)} %pad_add_fusion.1.info_ref, bf16[128,1536]{1,0:T(8,128)(2,1)} %get-tuple-element.140.attn_ref, bf16[384,1536]{1,0:T(8,128)(2,1)S(1)} %copy-done.3, ...), custom_call_target="tpu_custom_call" | custom-call | flops 5175000064 | tf_op jit(solution)/shard_map/branch_and_router/pallas_call | solution.py:444
  98.2 8.2 %experts_forward.2 = (f32[128,1536]{1,0:T(8,128)}, bf16[128,1536]{1,0:T(8,128)(2,1)S(1)}, bf16[2,256,1152]{2,1,0:T(8,128)(2,1)}, bf16[2,256,1152]{2,1,0:T(8,128)(2,1)}, bf16[256,1152]{1,0:T(8,128)(2,1)}) custom-call(s32[3]{0:T(128)S(1)} %pad_add_fusion.1.info_ref, bf16[128,1664]{1,0:T(8,128)(2,1)S(1)} %get-tuple-element.92.xa_ref.refs_8_.refs_0_.refs_4_, ...), custom_call_target="tpu_custom_call" | custom-call | flops 9200000000 | tf_op jit(solution)/shard_map/experts_forward/pallas_call | solution.py:644
  108.4 7.7 %experts_forward.3 = (f32[128,1536]{1,0:T(8,128)}, bf16[128,1536]{1,0:T(8,128)(2,1)S(1)}, bf16[2,256,1152]{2,1,0:T(8,128)(2,1)}, bf16[2,256,1152]{2,1,0:T(8,128)(2,1)}, bf16[256,1152]{1,0:T(8,128)(2,1)}) custom-call(s32[3]{0:T(128)S(1)} %pad_add_fusion.1.info_ref, bf16[128,1664]{1,0:T(8,128)(2,1)S(1)} %collective-permute-done.26.xa_ref.refs_10_.refs_2_, ...), custom_call_target="tpu_custom_call" | custom-call | flops 9200000000 | tf_op jit(solution)/shard_map/experts_forward/pallas_call | solution.py:644
  117.8 2.0 add_convert_fusion.1
  121.8 6.6 %collective-permute-done.31.x2.e2.refs_6_ = bf16[128,1664]{1,0:T(8,128)(2,1)} collective-permute-done((bf16[128,1664]{1,0:T(8,128)(2,1)S(1)}, bf16[128,1664]{1,0:T(8,128)(2,1)}, u32[]{:S(2)}, u32[]{:S(2)}) %collective-permute-start.31) | collective-permute-done | bytes 426016 | tf_op jit(solution)/shard_map/ppermute | solution.py:38
  131.3 4.2 result_and_error.1
  137.7 9.3 %pair_forward.1 = (bf16[512,1152]{1,0:T(8,128)(2,1)}, bf16[512,1152]{1,0:T(8,128)(2,1)}, bf16[512,1152]{1,0:T(8,128)(2,1)}) custom-call(s32[3]{0:T(128)S(1)} %pad_add_fusion.1.info_ref, bf16[1536,768]{1,0:T(8,128)(2,1)S(1)} %pad_maximum_fusion.shared_ref.refs_0_, bf16[4,1536,512]{2,1,0:T(8,128)(2,1)} %refs_1_.1, bf16[4,1536,512]{2,1,0:T(8,128)(2,1)} %refs_2_.1, ...), custom_call_target="tpu_custom_call" | custom-call | flops 9200000000 | tf_op jit(solution)/shard_map/pair_forward/pallas_call | solution.py:847
  149.0 8.6 %collective-permute-done.39.refs_6_.g2 = bf16[128,1664]{1,0:T(8,128)(2,1)S(1)} collective-permute-done((bf16[128,1664]{1,0:T(8,128)(2,1)S(1)}, bf16[128,1664]{1,0:T(8,128)(2,1)S(1)}, u32[]{:S(2)}, u32[]{:S(2)}) %collective-permute-start.39) | collective-permute-done | bytes 426016 | tf_op jit(solution)/shard_map/ppermute | solution.py:38
  160.2 8.5 %weight_gradients.2 = bf16[1536,1152]{1,0:T(8,128)(2,1)} custom-call(bf16[128,1664]{1,0:T(8,128)(2,1)} %copy-done.7, bf16[128,1664]{1,0:T(8,128)(2,1)} %copy-done.72, bf16[128,1664]{1,0:T(8,128)(2,1)} %copy-done.69, bf16[128,1664]{1,0:T(8,128)(2,1)} %copy-done.73, bf16[128,1664]{1,0:T(8,128)(2,1)} %copy-done.67, bf16[128,1664]{1,0:T(8,128)(2,1)} %copy-done.70, ...), custom_call_target="tpu_custom_call" | custom-call | flops 9200000000 | tf_op jit(solution)/shard_map/weight_gradients/pallas_call | solution.py:964
  168.8 21.2 %experts_backward.1 = (f32[128,1664]{1,0:T(8,128)}, bf16[128,1664]{1,0:T(8,128)(2,1)}, f32[128,1664]{1,0:T(8,128)S(1)}, bf16[128,1664]{1,0:T(8,128)(2,1)S(1)}, b...) custom-call(s32[3]{0:T(128)S(1)} %pad_add_fusion.1.info_ref, ...), custom_call_target="tpu_custom_call" | custom-call | flops 27599998976 | tf_op jit(solution)/shard_map/experts_backward/pallas_call | solution.py:771
  192.6 8.7 %pair_backward.1 = (bf16[512,1152]{1,0:T(8,128)(2,1)}, bf16[512,1152]{1,0:T(8,128)(2,1)}) custom-call(s32[3]{0:T(128)S(1)} %pad_add_fusion.1.info_ref, bf16[1536,768]{1,0:T(8,128)(2,1)S(1)} %pad_maximum_fusion.shared_ref.refs_0_, bf16[4,1536,512]{2,1,0:T(8,128)(2,1)} %down_in.1, bf16[128,1664]{1,0:T(8,128)(2,1)} %copy-done.67, bf16[128,1664]{1,0:T(8,128)(2,1)} %copy-done.70, ...), custom_call_target="tpu_custom_call" | custom-call | flops 8049999872 | tf_op jit(solution)/shard_map/pair_backward/pallas_call | solution.py:902
  201.3 2.5 collective-permute-done.42.far_ref
  204.5 14.4 %weight_gradients.3 = bf16[1536,2304]{1,0:T(8,128)(2,1)} custom-call(bf16[128,1664]{1,0:T(8,128)(2,1)} %copy-done.10, bf16[128,1664]{1,0:T(8,128)(2,1)} %copy-done.11, bf16[128,1664]{1,0:T(8,128)(2,1)} %copy-done.12, bf16[128,1664]{1,0:T(8,128)(2,1)} %copy-done.13, bf16[128,1664]{1,0:T(8,128)(2,1)} %collective-permute-done.27.x0.e0.refs_4_, ...), custom_call_target="tpu_custom_call" | custom-call | flops 18400000000 | tf_op jit(solution)/shard_map/weight_gradients/pallas_call | solution.py:964
  218.9 5.2 %residual_backward.1 = (f32[128,1536]{1,0:T(8,128)}, bf16[128,1536]{1,0:T(8,128)(2,1)S(1)}, bf16[128,1536]{1,0:T(8,128)(2,1)S(1)}, f32[24,1536]{1,0:T(8,128)S(1)}) custom-call(s32[3]{0:T(128)S(1)} %pad_add_fusion.1.info_ref, bf16[128,1664]{1,0:T(8,128)(2,1)S(1)} %copy-done.15, f32[1,1536]{1,0:T(1,128)S(1)} %maximum_convert_fusion.6.gain_ref, ...), custom_call_target="tpu_custom_call" | custom-call | flops 5750000128 | tf_op jit(solution)/shard_map/residual_backward/pallas_call | solution.py:563
  224.1 10.2 %attention_backward.1 = (bf16[128,1536]{1,0:T(8,128)(2,1)S(1)}, bf16[128,1024]{1,0:T(8,128)(2,1)S(1)}, bf16[128,1024]{1,0:T(8,128)(2,1)S(1)}, bf16[128,1024]{1,0...) custom-call(bf16[128,1536]{1,0:T(8,128)(2,1)S(1)} %get-tuple-element, ...), custom_call_target="tpu_custom_call" | custom-call | flops 11500000256 | tf_op jit(solution)/shard_map/attention_backward/pallas_call | solution.py:381
  234.3 5.8 %reduce-scatter.4.cloned.1.call-done = bf16[384,1152]{1,0:T(8,128)(2,1)} async-done(((bf16[1536,1152]{1,0:T(8,128)(2,1)}), bf16[384,1152]{1,0:T(8,128)(2,1)}) %reduce-scatter.4.cloned.1.call-update) | async-done | bytes 884752 | tf_op jit(solution)/shard_map/reduce_scatter | solution.py:1019
  253.0 5.5 %collective-permute-done.50 = bf16[128,1536]{1,0:T(8,128)(2,1)} collective-permute-done((bf16[128,1536]{1,0:T(8,128)(2,1)}, bf16[128,1536]{1,0:T(8,128)(2,1)}, u32[]{:S(2)}, u32[]{:S(2)}) %collective-permute-start.50) | collective-permute-done | bytes 393248 | tf_op jit(solution)/shard_map/ppermute | solution.py:38
  260.1 9.0 %collective-permute-done.57 = bf16[256,1024]{1,0:T(8,128)(2,1)S(1)} collective-permute-done((bf16[256,1024]{1,0:T(8,128)(2,1)}, bf16[256,1024]{1,0:T(8,128)(2,1)S(1)}, u32[]{:S(2)}, u32[]{:S(2)}) %collective-permute-start.57) | collective-permute-done | bytes 524320 | tf_op jit(solution)/shard_map/ppermute | solution.py:38
  271.5 2.8 collective-permute-done.48
  274.2 1.9 collective-permute-start.59
  276.1 2.1 convolution_convert_fusion.1
  278.3 9.5 %collective-permute-done.59 = bf16[128,1536]{1,0:T(8,128)(2,1)S(1)} collective-permute-done((bf16[128,1536]{1,0:T(8,128)(2,1)S(1)}, bf16[128,1536]{1,0:T(8,128)(2,1)S(1)}, u32[]{:S(2)}, u32[]{:S(2)}) %collective-permute-start.59) | collective-permute-done | bytes 393248 | tf_op jit(solution)/shard_map/ppermute | solution.py:38
  296.2 8.4 %collective-permute-done.52 = bf16[4,48,1536]{2,1,0:T(8,128)(2,1)S(1)} collective-permute-done((bf16[4,48,1536]{2,1,0:T(8,128)(2,1)S(1)}, bf16[4,48,1536]{2,1,0:T(8,128)(2,1)S(1)}, u32[]{:S(2)}, u32[]{:S(2)}) %collective-permute-start.52) | collective-permute-done | bytes 589856 | tf_op jit(solution)/shard_map/ppermute | solution.py:38
  304.8 4.2 collective-permute-done.45
  309.7 7.5 %collective-permute-done.61 = bf16[4,48,1536]{2,1,0:T(8,128)(2,1)S(1)} collective-permute-done((bf16[4,48,1536]{2,1,0:T(8,128)(2,1)S(1)}, bf16[4,48,1536]{2,1,0:T(8,128)(2,1)S(1)}, u32[]{:S(2)}, u32[]{:S(2)}) %collective-permute-start.61) | collective-permute-done | bytes 589856 | tf_op jit(solution)/shard_map/ppermute | solution.py:38
  317.4 10.6 %collective-permute-done.53 = bf16[128,1024]{1,0:T(8,128)(2,1)S(1)} collective-permute-done((bf16[128,1024]{1,0:T(8,128)(2,1)S(1)}, bf16[128,1024]{1,0:T(8,128)(2,1)S(1)}, u32[]{:S(2)}, u32[]{:S(2)}) %collective-permute-start.53) | collective-permute-done | bytes 262176 | tf_op jit(solution)/shard_map/ppermute | solution.py:1007
  330.2 6.6 %collective-permute-done.64 = bf16[128,1024]{1,0:T(8,128)(2,1)S(1)} collective-permute-done((bf16[128,1024]{1,0:T(8,128)(2,1)S(1)}, bf16[128,1024]{1,0:T(8,128)(2,1)S(1)}, u32[]{:S(2)}, u32[]{:S(2)}) %collective-permute-start.64) | collective-permute-done | bytes 262176 | tf_op jit(solution)/shard_map/ppermute | solution.py:38
  339.7 5.7 %collective-permute-done.65 = bf16[128,768]{1,0:T(8,128)(2,1)S(1)} collective-permute-done((bf16[128,768]{1,0:T(8,128)(2,1)S(1)}, bf16[128,768]{1,0:T(8,128)(2,1)S(1)}, u32[]{:S(2)}, u32[]{:S(2)}) %collective-permute-start.65) | collective-permute-done | bytes 196640 | tf_op jit(solution)/shard_map/ppermute | solution.py:38
  347.7 1.9 convolution_convert_fusion.2
  354.5 4.8 %collective-permute-done.68 = bf16[4,48,1024]{2,1,0:T(8,128)(2,1)} collective-permute-done((bf16[4,48,1024]{2,1,0:T(8,128)(2,1)S(1)}, bf16[4,48,1024]{2,1,0:T(8,128)(2,1)}, u32[]{:S(2)}, u32[]{:S(2)}) %collective-permute-start.68) | collective-permute-done | bytes 393248 | tf_op jit(solution)/shard_map/ppermute | solution.py:38
  362.4 3.7 collective-permute-done.72
  366.1 17.4 %collective-permute-start.73 = (f32[19,48]{1,0:T(8,128)S(1)}, f32[19,48]{1,0:T(8,128)S(1)}, u32[]{:S(2)}, u32[]{:S(2)}) collective-permute-start(f32[19,48]{1,0:T(8,128)S(1)} %bitcast.226), channel_id=1, source_target_pairs={{0,8},{4,12},{8,0},{12,4},{16,24},{20,28},{24,16},{28,20},{1,9},{5... | collective-permute-start | bytes 10952 | tf_op jit(solution)/shard_map/ppermute | solution.py:38
  383.6 2.4 collective-permute-start.75
  386.0 2.1 constant_dynamic-slice_fusion.3
  389.1 2.4 fusion.29
  393.8 13.2 %collective-permute-done.76 = bf16[192,2304]{1,0:T(8,128)(2,1)} collective-permute-done((bf16[192,2304]{1,0:T(8,128)(2,1)}, bf16[192,2304]{1,0:T(8,128)(2,1)}, u32[]{:S(2)}, u32[]{:S(2)}) %collective-permute-start.76) | collective-permute-done | bytes 884768 | tf_op jit(solution)/shard_map/ppermute | solution.py:38
  417.8 13.4 %reduce-scatter.8.cloned.1.call-done = bf16[48,4096]{1,0:T(8,128)(2,1)} async-done(((bf16[192,4096]{1,0:T(8,128)(2,1)}), bf16[48,4096]{1,0:T(8,128)(2,1)}) %reduce-scatter.8.cloned.1.call-update) | async-done | bytes 393232 | tf_op jit(solution)/shard_map/reduce_scatter | solution.py:1019
  431.2 1.8 fusion.70
  (442 shorter events, 111.0 us)
Async XLA Ops:
  7.2 232.9 %reduce-scatter.4.cloned.1.call-start = ((), (), s32[]{:S(2)}) async-start(), calls=%async_computation.3 | async-start | bytes 4423680 | tf_op jit(solution)/shard_map/reduce_scatter | solution.py:1019
  9.5 14.7 %collective-permute-start.2 = (bf16[18,384]{1,0:T(8,128)(2,1)S(1)}, bf16[18,384]{1,0:T(8,128)(2,1)S(1)}, u32[]{:S(2)}, u32[]{:S(2)}) collective-permute-start(bf16[18,384]{1,0:T(8,128)(2,1)S(1)} %pad_maximum_fusion.19), channel_id=1, source_target_pairs={{0,1},{1,0},{2,3},{3,2},{4,5},{5,4},{6,7},{7,6},{8,9},{9,8},{10,11... | collective-permute-start | bytes 41480 | tf_op jit(solution)/shard_map/ppermute | solution.py:38
  10.0 14.2 %collective-permute-start.6 = (bf16[18,384]{1,0:T(8,128)(2,1)S(1)}, bf16[18,384]{1,0:T(8,128)(2,1)S(1)}, u32[]{:S(2)}, u32[]{:S(2)}) collective-permute-start(bf16[18,384]{1,0:T(8,128)(2,1)S(1)} %pad_maximum_fusion.19), channel_id=1, source_target_pairs={{0,2},{1,3},{2,0},{3,1},{4,6},{5,7},{6,4},{7,5},{8,10},{9,11},{10,... | collective-permute-start | bytes 41480 | tf_op jit(solution)/shard_map/ppermute | solution.py:38
  24.2 23.6 %collective-permute-start.3 = (bf16[384,1536]{1,0:T(8,128)(2,1)S(1)}, bf16[384,1536]{1,0:T(8,128)(2,1)S(1)}, u32[]{:S(2)}, u32[]{:S(2)}) collective-permute-start(bf16[384,1536]{1,0:T(8,128)(2,1)S(1)} %copy-done.24), channel_id=1, source_target_pairs={{0,1},{1,0},{2,3},{3,2},{4,5},{5,4},{6,7},{7,6},{8,9},{9,8},{10,11... | collective-permute-start | bytes 3538952 | tf_op jit(solution)/shard_map/ppermute | solution.py:38
  36.6 14.5 %collective-permute-start.17 = (bf16[384,768]{1,0:T(8,128)(2,1)S(1)}, bf16[384,768]{1,0:T(8,128)(2,1)S(1)}, u32[]{:S(2)}, u32[]{:S(2)}) collective-permute-start(bf16[384,768]{1,0:T(8,128)(2,1)S(1)} %copy-done.44), channel_id=1, source_target_pairs={{0,2},{1,3},{2,0},{3,1},{4,6},{5,7},{6,4},{7,5},{8,10},{9,11},{10,... | collective-permute-start | bytes 1769480 | tf_op jit(solution)/shard_map/ppermute | solution.py:38
  37.6 15.8 %collective-permute-start.10 = (bf16[128,1024]{1,0:T(8,128)(2,1)S(1)}, bf16[128,1024]{1,0:T(8,128)(2,1)S(1)}, u32[]{:S(2)}, u32[]{:S(2)}) collective-permute-start(bf16[128,1024]{1,0:T(8,128)(2,1)S(1)} %fusion.39.refs_0_), channel_id=1, source_target_pairs={{0,8},{4,12},{8,16},{12,20},{16,24},{20,28},{1,9},{5,13},{9,17},{1... | collective-permute-start | bytes 786440 | tf_op jit(solution)/shard_map/ppermute | solution.py:993
  41.3 12.8 %collective-permute-start.12 = (bf16[128,1024]{1,0:T(8,128)(2,1)S(1)}, bf16[128,1024]{1,0:T(8,128)(2,1)S(1)}, u32[]{:S(2)}, u32[]{:S(2)}) collective-permute-start(bf16[128,1024]{1,0:T(8,128)(2,1)S(1)} %fusion.39.refs_0_), channel_id=1, source_target_pairs={{0,16},{4,20},{8,24},{12,28},{1,17},{5,21},{9,25},{13,29},{2,18},{... | collective-permute-start | bytes 786440 | tf_op jit(solution)/shard_map/ppermute | solution.py:993
  45.9 12.8 %collective-permute-start.14 = (bf16[128,1024]{1,0:T(8,128)(2,1)S(1)}, bf16[128,1024]{1,0:T(8,128)(2,1)S(1)}, u32[]{:S(2)}, u32[]{:S(2)}) collective-permute-start(bf16[128,1024]{1,0:T(8,128)(2,1)S(1)} %fusion.39.refs_0_), channel_id=1, source_target_pairs={{0,24},{4,28},{1,25},{5,29},{2,26},{6,30},{3,27},{7,31}} | collective-permute-start | bytes 786440 | tf_op jit(solution)/shard_map/ppermute | solution.py:993
  47.7 12.4 %collective-permute-start.9 = (bf16[128,1024]{1,0:T(8,128)(2,1)S(1)}, bf16[128,1024]{1,0:T(8,128)(2,1)S(1)}, u32[]{:S(2)}, u32[]{:S(2)}) collective-permute-start(bf16[128,1024]{1,0:T(8,128)(2,1)S(1)} %fusion.39.refs_0_), channel_id=1, source_target_pairs={{0,4},{4,0},{8,12},{12,8},{16,20},{20,16},{24,28},{28,24},{1,5},{5... | collective-permute-start | bytes 786440 | tf_op jit(solution)/shard_map/ppermute | solution.py:38
  51.1 18.9 %collective-permute-start.18 = (bf16[384,768]{1,0:T(8,128)(2,1)S(1)}, bf16[384,768]{1,0:T(8,128)(2,1)S(1)}, u32[]{:S(2)}, u32[]{:S(2)}) collective-permute-start(bf16[384,768]{1,0:T(8,128)(2,1)S(1)} %collective-permute-done.17), channel_id=1, source_target_pairs={{0,8},{4,12},{8,0},{12,4},{16,24},{20,28},{24,16},{28,20},{1,9},{5... | collective-permute-start | bytes 1769480 | tf_op jit(solution)/shard_map/ppermute | solution.py:38
  54.2 15.9 %collective-permute-start.11 = (bf16[128,1024]{1,0:T(8,128)(2,1)S(1)}, bf16[128,1024]{1,0:T(8,128)(2,1)S(1)}, u32[]{:S(2)}, u32[]{:S(2)}) collective-permute-start(bf16[128,1024]{1,0:T(8,128)(2,1)S(1)} %collective-permute-done.10.refs_2_), channel_id=1, source_target_pairs={{0,4},{4,0},{8,12},{12,8},{16,20},{20,16},{24,28},{28,24},{1,5},{5... | collective-permute-start | bytes 786440 | tf_op jit(solution)/shard_map/ppermute | solution.py:38
  58.7 12.0 %collective-permute-start.13 = (bf16[128,1024]{1,0:T(8,128)(2,1)S(1)}, bf16[128,1024]{1,0:T(8,128)(2,1)S(1)}, u32[]{:S(2)}, u32[]{:S(2)}) collective-permute-start(bf16[128,1024]{1,0:T(8,128)(2,1)S(1)} %collective-permute-done.12.refs_4_), channel_id=1, source_target_pairs={{0,4},{4,0},{8,12},{12,8},{16,20},{20,16},{24,28},{28,24},{1,5},{5... | collective-permute-start | bytes 786440 | tf_op jit(solution)/shard_map/ppermute | solution.py:38
  60.2 11.7 %collective-permute-start.15 = (bf16[128,1024]{1,0:T(8,128)(2,1)S(1)}, bf16[128,1024]{1,0:T(8,128)(2,1)S(1)}, u32[]{:S(2)}, u32[]{:S(2)}) collective-permute-start(bf16[128,1024]{1,0:T(8,128)(2,1)S(1)} %collective-permute-done.14.refs_6_), channel_id=1, source_target_pairs={{0,4},{4,0},{8,12},{12,8},{16,20},{20,16},{24,28},{28,24},{1,5},{5... | collective-permute-start | bytes 786440 | tf_op jit(solution)/shard_map/ppermute | solution.py:38
  62.7 25.1 %collective-permute-start.22 = (bf16[768,768]{1,0:T(8,128)(2,1)S(1)}, bf16[768,768]{1,0:T(8,128)(2,1)S(1)}, u32[]{:S(2)}, u32[]{:S(2)}) collective-permute-start(bf16[768,768]{1,0:T(8,128)(2,1)S(1)} %maximum_maximum_fusion), channel_id=1, source_target_pairs={{0,2},{1,3},{2,0},{3,1},{4,6},{5,7},{6,4},{7,5},{8,10},{9,11},{10,... | collective-permute-start | bytes 3538952 | tf_op jit(solution)/shard_map/ppermute | solution.py:38
  70.0 18.1 %collective-permute-start.16 = (bf16[384,1536]{1,0:T(8,128)(2,1)S(1)}, bf16[384,1536]{1,0:T(8,128)(2,1)S(1)}, u32[]{:S(2)}, u32[]{:S(2)}) collective-permute-start(bf16[384,1536]{1,0:T(8,128)(2,1)S(1)} %copy-done.3), channel_id=1, source_target_pairs={{0,1},{1,0},{2,3},{3,2},{4,5},{5,4},{6,7},{7,6},{8,9},{9,8},{10,11... | collective-permute-start | bytes 3538952 | tf_op jit(solution)/shard_map/ppermute | solution.py:38
  70.0 25.2 %collective-permute-start.24 = (bf16[384,768]{1,0:T(8,128)(2,1)S(1)}, bf16[384,768]{1,0:T(8,128)(2,1)S(1)}, u32[]{:S(2)}, u32[]{:S(2)}) collective-permute-start(bf16[384,768]{1,0:T(8,128)(2,1)S(1)} %pad_maximum_fusion.3), channel_id=1, source_target_pairs={{0,1},{1,0},{2,3},{3,2},{4,5},{5,4},{6,7},{7,6},{8,9},{9,8},{10,11... | collective-permute-start | bytes 1769480 | tf_op jit(solution)/shard_map/ppermute | solution.py:38
  71.9 16.2 %collective-permute-start.19 = (bf16[768,768]{1,0:T(8,128)(2,1)S(1)}, bf16[768,768]{1,0:T(8,128)(2,1)S(1)}, u32[]{:S(2)}, u32[]{:S(2)}) collective-permute-start(bf16[768,768]{1,0:T(8,128)(2,1)S(1)} %constant_dynamic-update-slice_fusion.o2.refs_9_), channel_id=1, source_target_pairs={{0,1},{1,0},{2,3},{3,2},{4,5},{5,4},{6,7},{7,6},{8,9},{9,8},{10,11... | collective-permute-start | bytes 3538952 | tf_op jit(solution)/shard_map/ppermute | solution.py:38
  93.2 13.3 %collective-permute-start.26 = (bf16[128,1664]{1,0:T(8,128)(2,1)S(1)}, bf16[128,1664]{1,0:T(8,128)(2,1)S(1)}, u32[]{:S(2)}, u32[]{:S(2)}) collective-permute-start(bf16[128,1664]{1,0:T(8,128)(2,1)S(1)} %get-tuple-element.92.xa_ref.refs_8_.refs_0_.refs_4_), channel_id=1, source_target_pairs={{0,2},{1,3},{2,0},{3,1},{4,6},{5,7},{6,4},{7,5},{8,10},{9,11},{10,... | collective-permute-start | bytes 1277960 | tf_op jit(solution)/shard_map/ppermute | solution.py:38
  93.7 12.8 %collective-permute-start.27 = (bf16[128,1664]{1,0:T(8,128)(2,1)S(1)}, bf16[128,1664]{1,0:T(8,128)(2,1)}, u32[]{:S(2)}, u32[]{:S(2)}) collective-permute-start(bf16[128,1664]{1,0:T(8,128)(2,1)S(1)} %get-tuple-element.92.xa_ref.refs_8_.refs_0_.refs_4_), channel_id=1, source_target_pairs={{0,4},{4,0},{8,12},{12,8},{16,20},{20,16},{24,28},{28,24},{1,5},{5... | collective-permute-start | bytes 1277960 | tf_op jit(solution)/shard_map/ppermute | solution.py:38
  116.2 12.2 %collective-permute-start.31 = (bf16[128,1664]{1,0:T(8,128)(2,1)S(1)}, bf16[128,1664]{1,0:T(8,128)(2,1)}, u32[]{:S(2)}, u32[]{:S(2)}) collective-permute-start(bf16[128,1664]{1,0:T(8,128)(2,1)S(1)} %collective-permute-done.26.xa_ref.refs_10_.refs_2_), channel_id=1, source_target_pairs={{0,4},{4,0},{8,12},{12,8},{16,20},{20,16},{24,28},{28,24},{1,5},{5... | collective-permute-start | bytes 1277960 | tf_op jit(solution)/shard_map/ppermute | solution.py:38
  119.8 11.5 %collective-permute-start.30 = (bf16[128,1536]{1,0:T(8,128)(2,1)}, bf16[128,1536]{1,0:T(8,128)(2,1)}, u32[]{:S(2)}, u32[]{:S(2)}) collective-permute-start(bf16[128,1536]{1,0:T(8,128)(2,1)} %add_convert_fusion.1), channel_id=1, source_target_pairs={{0,2},{1,3},{2,0},{3,1},{4,6},{5,7},{6,4},{7,5},{8,10},{9,11},{10,... | collective-permute-start | bytes 1179656 | tf_op jit(solution)/shard_map/ppermute | solution.py:38
  121.3 16.3 %collective-permute-start.35 = (bf16[128,1664]{1,0:T(8,128)(2,1)}, bf16[128,1664]{1,0:T(8,128)(2,1)}, u32[]{:S(2)}, u32[]{:S(2)}) collective-permute-start(bf16[128,1664]{1,0:T(8,128)(2,1)} %collective-permute-done.27.x0.e0.refs_4_), channel_id=1, source_target_pairs={{0,1},{1,0},{2,3},{3,2},{4,5},{5,4},{6,7},{7,6},{8,9},{9,8},{10,11... | collective-permute-start | bytes 1277960 | tf_op jit(solution)/shard_map/ppermute | solution.py:38
  135.5 11.5 %collective-permute-start.33 = (bf16[128,1664]{1,0:T(8,128)(2,1)S(1)}, bf16[128,1664]{1,0:T(8,128)(2,1)S(1)}, u32[]{:S(2)}, u32[]{:S(2)}) collective-permute-start(bf16[128,1664]{1,0:T(8,128)(2,1)S(1)} %get-tuple-element.111.refs_0_.refs_4_), channel_id=1, source_target_pairs={{0,2},{1,3},{2,0},{3,1},{4,6},{5,7},{6,4},{7,5},{8,10},{9,11},{10,... | collective-permute-start | bytes 1277960 | tf_op jit(solution)/shard_map/ppermute | solution.py:38
  137.0 10.8 %collective-permute-start.34 = (bf16[128,1664]{1,0:T(8,128)(2,1)S(1)}, bf16[128,1664]{1,0:T(8,128)(2,1)S(1)}, u32[]{:S(2)}, u32[]{:S(2)}) collective-permute-start(bf16[128,1664]{1,0:T(8,128)(2,1)S(1)} %get-tuple-element.111.refs_0_.refs_4_), channel_id=1, source_target_pairs={{0,4},{4,0},{8,12},{12,8},{16,20},{20,16},{24,28},{28,24},{1,5},{5... | collective-permute-start | bytes 1277960 | tf_op jit(solution)/shard_map/ppermute | solution.py:38
  168.7 217.3 %reduce-scatter.6.cloned.1.call-start = ((), (), s32[]{:S(2)}) async-start(), calls=%async_computation.4 | async-start | bytes 8847360 | tf_op jit(solution)/shard_map/reduce_scatter | solution.py:1019
  190.1 28.8 %collective-permute-start.43 = (bf16[128,1664]{1,0:T(8,128)(2,1)}, bf16[128,1664]{1,0:T(8,128)(2,1)}, u32[]{:S(2)}, u32[]{:S(2)}) collective-permute-start(bf16[128,1664]{1,0:T(8,128)(2,1)} %get-tuple-element.128), channel_id=1, source_target_pairs={{0,1},{1,0},{2,3},{3,2},{4,5},{5,4},{6,7},{7,6},{8,9},{9,8},{10,11... | collective-permute-start | bytes 1277960 | tf_op jit(solution)/shard_map/ppermute | solution.py:38
  191.9 11.9 %collective-permute-start.42 = (bf16[128,1664]{1,0:T(8,128)(2,1)S(1)}, bf16[128,1664]{1,0:T(8,128)(2,1)S(1)}, u32[]{:S(2)}, u32[]{:S(2)}) collective-permute-start(bf16[128,1664]{1,0:T(8,128)(2,1)S(1)} %add_convert_fusion), channel_id=1, source_target_pairs={{0,2},{1,3},{2,0},{3,1},{4,6},{5,7},{6,4},{7,5},{8,10},{9,11},{10,... | collective-permute-start | bytes 1277960 | tf_op jit(solution)/shard_map/ppermute | solution.py:38
  240.2 191.0 %reduce-scatter.8.cloned.1.call-start = ((), (), s32[]{:S(2)}) async-start(), calls=%async_computation.5 | async-start | bytes 1966080 | tf_op jit(solution)/shard_map/reduce_scatter | solution.py:1019
  244.2 15.8 %collective-permute-start.44 = (bf16[256,1024]{1,0:T(8,128)(2,1)}, bf16[256,1024]{1,0:T(8,128)(2,1)S(1)}, u32[]{:S(2)}, u32[]{:S(2)}) collective-permute-start(bf16[256,1024]{1,0:T(8,128)(2,1)} %pad_maximum_fusion.6), channel_id=1, source_target_pairs={{0,4},{4,0},{8,12},{12,8},{16,20},{20,16},{24,28},{28,24},{1,5},{5... | collective-permute-start | bytes 1572872 | tf_op jit(solution)/shard_map/ppermute | solution.py:38
  249.2 25.0 %collective-permute-start.49 = (bf16[128,1536]{1,0:T(8,128)(2,1)}, bf16[128,1536]{1,0:T(8,128)(2,1)}, u32[]{:S(2)}, u32[]{:S(2)}) collective-permute-start(bf16[128,1536]{1,0:T(8,128)(2,1)} %get-tuple-element.140.attn_ref), channel_id=1, source_target_pairs={{0,1},{1,0},{2,3},{3,2},{4,5},{5,4},{6,7},{7,6},{8,9},{9,8},{10,11... | collective-permute-start | bytes 1179656 | tf_op jit(solution)/shard_map/ppermute | solution.py:38
  250.3 18.8 %collective-permute-start.57 = (bf16[256,1024]{1,0:T(8,128)(2,1)}, bf16[256,1024]{1,0:T(8,128)(2,1)S(1)}, u32[]{:S(2)}, u32[]{:S(2)}) collective-permute-start(bf16[256,1024]{1,0:T(8,128)(2,1)} %pad_maximum_fusion.7), channel_id=1, source_target_pairs={{0,4},{4,0},{8,12},{12,8},{16,20},{20,16},{24,28},{28,24},{1,5},{5... | collective-permute-start | bytes 1572872 | tf_op jit(solution)/shard_map/ppermute | solution.py:38
  251.7 17.6 %collective-permute-start.46 = (bf16[128,384]{0,1:T(8,128)(2,1)}, bf16[128,384]{0,1:T(8,128)(2,1)}, u32[]{:S(2)}, u32[]{:S(2)}) collective-permute-start(bf16[128,384]{0,1:T(8,128)(2,1)} %get-tuple-element.211), channel_id=1, source_target_pairs={{0,1},{1,0},{2,3},{3,2},{4,5},{5,4},{6,7},{7,6},{8,9},{9,8},{10,11... | collective-permute-start | bytes 294920 | tf_op jit(solution)/shard_map/ppermute | solution.py:38
  258.5 12.4 %collective-permute-start.47 = (bf16[128,384]{0,1:T(8,128)(2,1)}, bf16[128,384]{0,1:T(8,128)(2,1)S(1)}, u32[]{:S(2)}, u32[]{:S(2)}) collective-permute-start(bf16[128,384]{0,1:T(8,128)(2,1)} %get-tuple-element.210), channel_id=1, source_target_pairs={{0,2},{1,3},{2,0},{3,1},{4,6},{5,7},{6,4},{7,5},{8,10},{9,11},{10,... | collective-permute-start | bytes 294920 | tf_op jit(solution)/shard_map/ppermute | solution.py:38
  259.9 16.2 %collective-permute-start.51 = (bf16[128,1536]{1,0:T(8,128)(2,1)}, bf16[128,1536]{1,0:T(8,128)(2,1)S(1)}, u32[]{:S(2)}, u32[]{:S(2)}) collective-permute-start(bf16[128,1536]{1,0:T(8,128)(2,1)} %collective-permute-done.50), channel_id=1, source_target_pairs={{0,1},{1,0},{2,3},{3,2},{4,5},{5,4},{6,7},{7,6},{8,9},{9,8},{10,11... | collective-permute-start | bytes 1179656 | tf_op jit(solution)/shard_map/ppermute | solution.py:38
  269.2 19.1 %collective-permute-start.54 = (bf16[128,384]{0,1:T(8,128)(2,1)S(1)}, bf16[128,384]{0,1:T(8,128)(2,1)S(1)}, u32[]{:S(2)}, u32[]{:S(2)}) collective-permute-start(bf16[128,384]{0,1:T(8,128)(2,1)S(1)} %copy-done.61), channel_id=1, source_target_pairs={{0,1},{1,0},{2,3},{3,2},{4,5},{5,4},{6,7},{7,6},{8,9},{9,8},{10,11... | collective-permute-start | bytes 294920 | tf_op jit(solution)/shard_map/ppermute | solution.py:38
  270.9 19.6 %collective-permute-start.55 = (bf16[128,384]{0,1:T(8,128)(2,1)S(1)}, bf16[128,384]{0,1:T(8,128)(2,1)S(1)}, u32[]{:S(2)}, u32[]{:S(2)}) collective-permute-start(bf16[128,384]{0,1:T(8,128)(2,1)S(1)} %copy-done.60), channel_id=1, source_target_pairs={{0,2},{1,3},{2,0},{3,1},{4,6},{5,7},{6,4},{7,5},{8,10},{9,11},{10,... | collective-permute-start | bytes 294920 | tf_op jit(solution)/shard_map/ppermute | solution.py:38
  274.2 17.6 %collective-permute-start.56 = (bf16[128,384]{0,1:T(8,128)(2,1)S(1)}, bf16[128,384]{0,1:T(8,128)(2,1)S(1)}, u32[]{:S(2)}, u32[]{:S(2)}) collective-permute-start(bf16[128,384]{0,1:T(8,128)(2,1)S(1)} %copy-done.59), channel_id=1, source_target_pairs={{0,3},{1,2},{2,1},{3,0},{4,7},{5,6},{6,5},{7,4},{8,11},{9,10},{10,... | collective-permute-start | bytes 294920 | tf_op jit(solution)/shard_map/ppermute | solution.py:38
  274.2 13.5 %collective-permute-start.59 = (bf16[128,1536]{1,0:T(8,128)(2,1)S(1)}, bf16[128,1536]{1,0:T(8,128)(2,1)S(1)}, u32[]{:S(2)}, u32[]{:S(2)}) collective-permute-start(bf16[128,1536]{1,0:T(8,128)(2,1)S(1)} %get-tuple-element.145), channel_id=1, source_target_pairs={{0,2},{1,3},{2,0},{3,1},{4,6},{5,7},{6,4},{7,5},{8,10},{9,11},{10,... | collective-permute-start | bytes 1179656 | tf_op jit(solution)/shard_map/ppermute | solution.py:38
  276.1 17.0 %collective-permute-start.58 = (bf16[128,1536]{1,0:T(8,128)(2,1)S(1)}, bf16[128,1536]{1,0:T(8,128)(2,1)S(1)}, u32[]{:S(2)}, u32[]{:S(2)}) collective-permute-start(bf16[128,1536]{1,0:T(8,128)(2,1)S(1)} %get-tuple-element.145), channel_id=1, source_target_pairs={{0,1},{1,0},{2,3},{3,2},{4,5},{5,4},{6,7},{7,6},{8,9},{9,8},{10,11... | collective-permute-start | bytes 1179656 | tf_op jit(solution)/shard_map/ppermute | solution.py:38
  288.4 16.2 %collective-permute-start.52 = (bf16[4,48,1536]{2,1,0:T(8,128)(2,1)S(1)}, bf16[4,48,1536]{2,1,0:T(8,128)(2,1)S(1)}, u32[]{:S(2)}, u32[]{:S(2)}) collective-permute-start(bf16[4,48,1536]{2,1,0:T(8,128)(2,1)S(1)} %dynamic-slice_bitcast_fusion.1), channel_id=1, source_target_pairs={{0,4},{4,0},{8,12},{12,8},{16,20},{20,16},{24,28},{28,24},{1,5},{5... | collective-permute-start | bytes 1769480 | tf_op jit(solution)/shard_map/ppermute | solution.py:38
  290.5 18.5 %collective-permute-start.45 = (bf16[128,1024]{1,0:T(8,128)(2,1)S(1)}, bf16[128,1024]{1,0:T(8,128)(2,1)S(1)}, u32[]{:S(2)}, u32[]{:S(2)}) collective-permute-start(bf16[128,1024]{1,0:T(8,128)(2,1)S(1)} %get-tuple-element.191), channel_id=1, source_target_pairs={{24,0},{28,4},{25,1},{29,5},{26,2},{30,6},{27,3},{31,7}} | collective-permute-start | bytes 786440 | tf_op jit(solution)/shard_map/ppermute | solution.py:1007
  291.9 36.2 %collective-permute-start.53 = (bf16[128,1024]{1,0:T(8,128)(2,1)S(1)}, bf16[128,1024]{1,0:T(8,128)(2,1)S(1)}, u32[]{:S(2)}, u32[]{:S(2)}) collective-permute-start(bf16[128,1024]{1,0:T(8,128)(2,1)S(1)} %get-tuple-element.192), channel_id=1, source_target_pairs={{16,0},{20,4},{24,8},{28,12},{17,1},{21,5},{25,9},{29,13},{18,2},{... | collective-permute-start | bytes 786440 | tf_op jit(solution)/shard_map/ppermute | solution.py:1007
  293.2 35.1 %collective-permute-start.62 = (bf16[128,1024]{1,0:T(8,128)(2,1)S(1)}, bf16[128,1024]{1,0:T(8,128)(2,1)S(1)}, u32[]{:S(2)}, u32[]{:S(2)}) collective-permute-start(bf16[128,1024]{1,0:T(8,128)(2,1)S(1)} %add_convert_fusion.3), channel_id=1, source_target_pairs={{8,0},{12,4},{16,8},{20,12},{24,16},{28,20},{9,1},{13,5},{17,9},{2... | collective-permute-start | bytes 786440 | tf_op jit(solution)/shard_map/ppermute | solution.py:1007
  295.5 21.7 %collective-permute-start.61 = (bf16[4,48,1536]{2,1,0:T(8,128)(2,1)S(1)}, bf16[4,48,1536]{2,1,0:T(8,128)(2,1)S(1)}, u32[]{:S(2)}, u32[]{:S(2)}) collective-permute-start(bf16[4,48,1536]{2,1,0:T(8,128)(2,1)S(1)} %dynamic-slice_bitcast_fusion), channel_id=1, source_target_pairs={{0,4},{4,0},{8,12},{12,8},{16,20},{20,16},{24,28},{28,24},{1,5},{5... | collective-permute-start | bytes 1769480 | tf_op jit(solution)/shard_map/ppermute | solution.py:38
  309.1 19.0 %collective-permute-start.63 = (bf16[192,1152]{1,0:T(8,128)(2,1)S(1)}, bf16[192,1152]{1,0:T(8,128)(2,1)S(1)}, u32[]{:S(2)}, u32[]{:S(2)}) collective-permute-start(bf16[192,1152]{1,0:T(8,128)(2,1)S(1)} %constant_dynamic-slice_fusion.14), channel_id=1, source_target_pairs={{0,4},{4,0},{8,12},{12,8},{16,20},{20,16},{24,28},{28,24},{1,5},{5... | collective-permute-start | bytes 1327112 | tf_op jit(solution)/shard_map/ppermute | solution.py:38
  328.6 19.2 %collective-permute-start.66 = (bf16[128,1024]{1,0:T(8,128)(2,1)S(1)}, bf16[128,1024]{1,0:T(8,128)(2,1)}, u32[]{:S(2)}, u32[]{:S(2)}) collective-permute-start(bf16[128,1024]{1,0:T(8,128)(2,1)S(1)} %add_convert_fusion.2), channel_id=1, source_target_pairs={{0,1},{1,0},{2,3},{3,2},{4,5},{5,4},{6,7},{7,6},{8,9},{9,8},{10,11... | collective-permute-start | bytes 786440 | tf_op jit(solution)/shard_map/ppermute | solution.py:38
  366.1 25.3 %collective-permute-start.73 = (f32[19,48]{1,0:T(8,128)S(1)}, f32[19,48]{1,0:T(8,128)S(1)}, u32[]{:S(2)}, u32[]{:S(2)}) collective-permute-start(f32[19,48]{1,0:T(8,128)S(1)} %bitcast.226), channel_id=1, source_target_pairs={{0,8},{4,12},{8,0},{12,4},{16,24},{20,28},{24,16},{28,20},{1,9},{5... | collective-permute-start | bytes 10952 | tf_op jit(solution)/shard_map/ppermute | solution.py:38
  388.1 18.9 %collective-permute-start.76 = (bf16[192,2304]{1,0:T(8,128)(2,1)}, bf16[192,2304]{1,0:T(8,128)(2,1)}, u32[]{:S(2)}, u32[]{:S(2)}) collective-permute-start(bf16[192,2304]{1,0:T(8,128)(2,1)} %constant_dynamic-slice_fusion.3), channel_id=1, source_target_pairs={{0,4},{4,0},{8,12},{12,8},{16,20},{20,16},{24,28},{28,24},{1,5},{5... | collective-permute-start | bytes 2654216 | tf_op jit(solution)/shard_map/ppermute | solution.py:38
  (118 other events, 1180.5 us)
Sparse Core Ops, SparseCore 0:
  168.8 71.2 reduce-scatter.3
  242.4 140.7 reduce-scatter.5
  393.4 37.7 reduce-scatter.7
